TPU v7x, 512 devices: a whole 4x8x8 slice. The times are simulated.
512 devices in a mesh: tm: 128 (over y, z, core), space: 4 (over x).
Axes of the slice: x: 4, y: 8, z: 8, core: 2. Of those that a mesh axis runs over, the one named last changes fastest.
Arguments:
- video: bfloat16 [128, 8, 8, 16, 128], P('tm', None, 'space'), may hold values from -6 to 6
- cotangent: bfloat16 [128, 8, 8, 16, 128], P('tm', None, 'space'), may hold values from -6 to 6
- weight_one: bfloat16 [3456, 128], replicated, may hold values from -0.109375 to 0.109375
- weight_two: bfloat16 [3456, 128], replicated, may hold values from -0.109375 to 0.109375
- predecessor: int32 [128], P('tm'), may hold values from -1 to 126, as said below
- frame_count: int32 [128], P('tm'), may hold values from 1 to 8, as said below
Outputs:
- output: bfloat16 [128, 8, 8, 16, 128], P('tm', None, 'space')
- grad_one: float32 [3456, 128], P('space')
- grad_two: float32 [3456, 128], P('space')
Inputs may be any that keep to these rules, and one draw needn't show every extreme that they name: predecessor[c] is c - 1, or -1 where group c starts a clip; group 0 starts a clip and group 1 continues it. `frame_count`: a group with fewer than 8 frames is the last group or is followed by a group that starts a clip; the last group has fewer than 8 frames.
All inputs are finite; a program needn't handle non-finite values.
Results may differ from a plain program's by a relative error of at most 0.006.
Values may be sent and summed in bfloat16 or wider, within the bound.
A program may use at most 64 MiB of HBM per device.

v0:
```python
import math

import jax
import jax.numpy as jnp
from jax import lax
from jax.sharding import PartitionSpec as P


def with_halo(cells, sides, width):
    for axis, dim in sides:
        count = lax.axis_size(axis)
        ends = count - 1
        head = lax.slice_in_dim(cells, 0, width, axis=dim)
        tail = lax.slice_in_dim(cells, cells.shape[dim] - width, cells.shape[dim], axis=dim)
        cells = jnp.concatenate(
            [
                lax.ppermute(tail, axis, [(i, (i + 1) % count) for i in range(ends)]),
                cells,
                lax.ppermute(head, axis, [((i + 1) % count, i) for i in range(ends)]),
            ],
            axis=dim,
        )
    return cells


def passed_along(value, axis, steps):
    count = lax.axis_size(axis)
    initial, last = (max(0, -steps), min(count, count - steps))
    return lax.ppermute(value, axis, [(source, source + steps) for source in range(initial, last)])


def build_patches(extended, frames, height, columns):
    pieces = []
    for depth in range(3):
        for down in range(3):
            for across in range(3):
                pieces.append(
                    extended[
                        depth : depth + frames, down : down + height, across : across + columns, :
                    ]
                )
    stacked = jnp.concatenate(pieces, axis=-1)
    return stacked.reshape(frames * height * columns, stacked.shape[-1])


def silu_slope(value):
    sigma = jax.nn.sigmoid(value)
    return sigma * (1.0 + value * (1.0 - sigma))


def contract(patches, delta):
    return lax.dot_general(
        patches, delta, (((0,), (0,)), ((), ())), preferred_element_type=jnp.float32
    )


def extend(field, starting):
    tall = with_halo(field, (("space", 1),), 1)
    earlier = passed_along(tall[tall.shape[0] - 2 :], "tm", 1)
    own_first = jnp.concatenate([tall[:1], tall[:1]], axis=0)
    cache = jnp.where(starting, own_first, earlier)
    joined = jnp.concatenate([cache, tall], axis=0)
    return jnp.pad(joined, ((0, 0), (0, 0), (1, 1), (0, 0)))


def share_rows(total):
    count = total.shape[0] // lax.axis_size("space")
    return lax.dynamic_slice_in_dim(total, lax.axis_index("space") * count, count, 0)


def per_device(video, cotangent, weight_one, weight_two, predecessor, frame_count):
    frames, height, columns, width = video.shape[1:]
    field = video[0]
    starting = predecessor[0] < 0
    live = (jnp.arange(frames) < frame_count[0]).astype(jnp.float32)[:, None, None, None]
    scale = 1.0 / math.sqrt(
        lax.axis_size("tm") * lax.axis_size("space") * frames * height * columns
    )
    patches_one = build_patches(extend(field, starting), frames, height, columns)
    first_act = jnp.dot(patches_one, weight_one, preferred_element_type=jnp.float32).reshape(
        frames, height, columns, width
    )
    hidden = (live * jax.nn.silu(first_act)).astype(jnp.bfloat16)
    ext_two = extend(hidden, starting)
    patches_two = build_patches(ext_two, frames, height, columns)
    second_act = jnp.dot(patches_two, weight_two, preferred_element_type=jnp.float32).reshape(
        frames, height, columns, width
    )
    output = (live * (field.astype(jnp.float32) + second_act)).astype(jnp.bfloat16)
    delta_two = (live * cotangent[0].astype(jnp.float32)).astype(jnp.bfloat16).reshape(-1, width)
    grad_two = scale * contract(patches_two, delta_two)
    back = lax.dot_general(
        delta_two, weight_two, (((1,), (1,)), ((), ())), preferred_element_type=jnp.float32
    )
    _, pull = jax.vjp(
        lambda grid: build_patches(grid, frames, height, columns),
        jnp.zeros(ext_two.shape, jnp.float32),
    )
    spread = pull(back)[0][:, :, 1 : columns + 1]
    from_below = passed_along(spread[:, :1].astype(jnp.bfloat16), "space", -1).astype(jnp.float32)
    from_above = passed_along(spread[:, height + 1 :].astype(jnp.bfloat16), "space", 1).astype(
        jnp.float32
    )
    inner = spread[:, 1 : height + 1]
    inner = inner.at[:, :1].add(from_above).at[:, height - 1 :].add(from_below)
    cache_part = inner[:2]
    own = inner[2:]
    passing = jnp.where(starting, 0.0, cache_part)
    from_next = passed_along(passing.astype(jnp.bfloat16), "tm", -1).astype(passing.dtype)
    own = own.at[frames - 2 :].add(from_next)
    own = own.at[0].add(jnp.where(starting, cache_part[0] + cache_part[1], 0.0))
    delta_one = (own * live * silu_slope(first_act)).astype(jnp.bfloat16).reshape(-1, width)
    grad_one = scale * contract(patches_one, delta_one)
    grad_one, grad_two = lax.psum((grad_one, grad_two), ("tm", "space"))
    grad_one = share_rows(grad_one)
    grad_two = share_rows(grad_two)
    return (output[None], grad_one, grad_two)


def solution(mesh):
    placed = (
        P("tm", None, "space", None, None),
        P("tm", None, "space", None, None),
        P(),
        P(),
        P("tm"),
        P("tm"),
    )
    return jax.shard_map(
        per_device,
        mesh=mesh,
        in_specs=placed,
        out_specs=(P("tm", None, "space", None, None), P("space", None), P("space", None)),
        check_vma=False,
    )
```

profile of v0, /device:TPU:1, one launch (start us, length us, event | category | flops | bytes accessed | tf_op | source)
XLA Modules:
  0.0 349.7 jit_solution(11779764848098692025)
XLA Ops:
  7.2 0.0 copy-start
  7.2 0.0 all-reduce.32.cloned.1.call-start
  7.2 0.9 fusion.28
  8.1 3.9 %collective-permute-start = (bf16[8,1,16,128]{3,2,1,0:T(8,128)(2,1)S(1)}, bf16[8,1,16,128]{3,2,1,0:T(8,128)(2,1)S(1)}, u32[]{:S(2)}, u32[]{:S(2)}) collective-permute-start(bf16[8,1,16,128]{3,2,1,0:T(8,128)(2,1)S(1)} %get-tuple-element.86), channel_id=1, source_target_pairs={{0,1},{1,2},{2,3},{4,5},{5,6},{6,7},{8,9},{9,10},{10,11},{12,13},{... | collective-permute-start | bytes 98312 | tf_op jit(solution)/shard_map/ppermute | solution.py:17
  12.0 1.3 collective-permute-start.1
  14.0 1.5 fusion.7
  15.5 0.3 fusion.24
  15.9 0.1 fusion.25
  16.0 0.0 copy-start.1
  16.0 0.4 fusion.23
  16.5 4.0 %collective-permute-start.6 = (bf16[10,1,16,128]{3,2,1,0:T(8,128)(2,1)S(1)}, bf16[10,1,16,128]{3,2,1,0:T(8,128)(2,1)S(1)}, u32[]{:S(2)}, u32[]{:S(2)}) collective-permute-start(bf16[10,1,16,128]{3,2,1,0:T(8,128)(2,1)S(1)} %get-tuple-element.83), channel_id=1, source_target_pairs={{0,1},{1,2},{2,3},{4,5},{5,6},{6,7},{8,9},{9,10},{10,11},{12,13},{... | collective-permute-start | bytes 122888 | tf_op jit(solution)/shard_map/ppermute | solution.py:29
  20.5 1.3 collective-permute-start.7
  22.5 0.0 collective-permute-done
  22.5 5.4 %collective-permute-start.2 = (bf16[2,4,16,128]{3,2,1,0:T(8,128)(2,1)S(1)}, bf16[2,4,16,128]{3,2,1,0:T(8,128)(2,1)S(1)}, u32[]{:S(2)}, u32[]{:S(2)}) collective-permute-start(bf16[2,4,16,128]{3,2,1,0:T(8,128)(2,1)S(1)} %pad_maximum_fusion.6), channel_id=1, source_target_pairs={{0,4},{4,8},{8,12},{12,16},{16,20},{20,24},{24,28},{28,32},{32,36}... | collective-permute-start | bytes 98312 | tf_op jit(solution)/shard_map/ppermute | solution.py:29
  28.0 5.1 %collective-permute-start.8 = (bf16[2,2,16,128]{3,2,1,0:T(8,128)(2,1)S(1)}, bf16[2,2,16,128]{3,2,1,0:T(8,128)(2,1)S(1)}, u32[]{:S(2)}, u32[]{:S(2)}) collective-permute-start(bf16[2,2,16,128]{3,2,1,0:T(8,128)(2,1)S(1)} %fusion.15), channel_id=1, source_target_pairs={{4,0},{8,4},{12,8},{16,12},{20,16},{24,20},{28,24},{32,28},{36,32}... | collective-permute-start | bytes 49160 | tf_op jit(solution)/shard_map/ppermute | solution.py:29
  33.2 0.8 collective-permute-done.8
  34.3 0.0 copy-start.3
  34.9 0.6 copy-done.3
  35.5 0.6 multiply_convert_fusion.1
  36.1 3.4 collective-permute-start.3
  39.5 1.3 collective-permute-start.4
  40.8 2.0 fusion.1
  42.8 1.4 collective-permute-done.4
  44.2 3.3 collective-permute-start.5
  47.6 1.0 collective-permute-done.5
  48.9 0.0 copy-start.2
  49.5 0.2 copy-done.2
  49.7 1.9 fusion
  51.7 0.0 all-reduce.32.cloned.1.call-update
  51.7 1.3 fusion.4
  53.0 287.8 %all-reduce.32.cloned.1.call-done = (f32[3456,128]{1,0:T(8,128)}, f32[3456,128]{1,0:T(8,128)}) async-done(((f32[3456,128]{1,0:T(8,128)}, f32[3456,128]{1,0:T(8,128)}), (f32[3456,128]{1,0:T(8,128)}, f32[3456,128]{1,0:T(8,128)})) %all-reduce.32.cloned.1.call-update) | async-done | bytes 3538960 | tf_op jit(solution)/shard_map/psum | solution.py:114
  340.7 2.1 constant_dynamic-slice_fusion
  (79 shorter events, 1.8 us)
Async XLA Ops:
  7.2 6.8 %copy-start = (bf16[3456,128]{1,0:T(8,128)(2,1)S(1)}, bf16[3456,128]{1,0:T(8,128)(2,1)}, u32[]{:S(2)}) copy-start(bf16[3456,128]{1,0:T(8,128)(2,1)} %param.17) | copy-start | bytes 2654212
  7.2 333.5 %all-reduce.32.cloned.1.call-start = ((), (), s32[]{:S(2)}) async-start(), calls=%async_computation | async-start | bytes 7077888 | tf_op jit(solution)/shard_map/psum | solution.py:114
  8.1 14.4 %collective-permute-start = (bf16[8,1,16,128]{3,2,1,0:T(8,128)(2,1)S(1)}, bf16[8,1,16,128]{3,2,1,0:T(8,128)(2,1)S(1)}, u32[]{:S(2)}, u32[]{:S(2)}) collective-permute-start(bf16[8,1,16,128]{3,2,1,0:T(8,128)(2,1)S(1)} %get-tuple-element.86), channel_id=1, source_target_pairs={{0,1},{1,2},{2,3},{4,5},{5,6},{6,7},{8,9},{9,10},{10,11},{12,13},{... | collective-permute-start | bytes 98312 | tf_op jit(solution)/shard_map/ppermute | solution.py:17
  12.0 10.5 %collective-permute-start.1 = (bf16[8,1,16,128]{3,2,1,0:T(8,128)(2,1)S(1)}, bf16[8,1,16,128]{3,2,1,0:T(8,128)(2,1)S(1)}, u32[]{:S(2)}, u32[]{:S(2)}) collective-permute-start(bf16[8,1,16,128]{3,2,1,0:T(8,128)(2,1)S(1)} %get-tuple-element.87), channel_id=1, source_target_pairs={{1,0},{2,1},{3,2},{5,4},{6,5},{7,6},{9,8},{10,9},{11,10},{13,12},{... | collective-permute-start | bytes 98312 | tf_op jit(solution)/shard_map/ppermute | solution.py:19
  16.0 6.5 %copy-start.1 = (bf16[1,8,2,16,128]{4,3,2,1,0:T(8,128)(2,1)S(1)}, bf16[1,8,2,16,128]{4,3,2,1,0:T(8,128)(2,1)}, u32[]{:S(2)}) copy-start(bf16[1,8,2,16,128]{4,3,2,1,0:T(8,128)(2,1)} %param.14) | copy-start | bytes 196612
  16.5 11.4 %collective-permute-start.6 = (bf16[10,1,16,128]{3,2,1,0:T(8,128)(2,1)S(1)}, bf16[10,1,16,128]{3,2,1,0:T(8,128)(2,1)S(1)}, u32[]{:S(2)}, u32[]{:S(2)}) collective-permute-start(bf16[10,1,16,128]{3,2,1,0:T(8,128)(2,1)S(1)} %get-tuple-element.83), channel_id=1, source_target_pairs={{0,1},{1,2},{2,3},{4,5},{5,6},{6,7},{8,9},{9,10},{10,11},{12,13},{... | collective-permute-start | bytes 122888 | tf_op jit(solution)/shard_map/ppermute | solution.py:29
  20.5 7.5 %collective-permute-start.7 = (bf16[10,1,16,128]{3,2,1,0:T(8,128)(2,1)S(1)}, bf16[10,1,16,128]{3,2,1,0:T(8,128)(2,1)S(1)}, u32[]{:S(2)}, u32[]{:S(2)}) collective-permute-start(bf16[10,1,16,128]{3,2,1,0:T(8,128)(2,1)S(1)} %get-tuple-element.82), channel_id=1, source_target_pairs={{1,0},{2,1},{3,2},{5,4},{6,5},{7,6},{9,8},{10,9},{11,10},{13,12},{... | collective-permute-start | bytes 122888 | tf_op jit(solution)/shard_map/ppermute | solution.py:29
  22.5 11.4 %collective-permute-start.2 = (bf16[2,4,16,128]{3,2,1,0:T(8,128)(2,1)S(1)}, bf16[2,4,16,128]{3,2,1,0:T(8,128)(2,1)S(1)}, u32[]{:S(2)}, u32[]{:S(2)}) collective-permute-start(bf16[2,4,16,128]{3,2,1,0:T(8,128)(2,1)S(1)} %pad_maximum_fusion.6), channel_id=1, source_target_pairs={{0,4},{4,8},{8,12},{12,16},{16,20},{20,24},{24,28},{28,32},{32,36}... | collective-permute-start | bytes 98312 | tf_op jit(solution)/shard_map/ppermute | solution.py:29
  28.0 5.9 %collective-permute-start.8 = (bf16[2,2,16,128]{3,2,1,0:T(8,128)(2,1)S(1)}, bf16[2,2,16,128]{3,2,1,0:T(8,128)(2,1)S(1)}, u32[]{:S(2)}, u32[]{:S(2)}) collective-permute-start(bf16[2,2,16,128]{3,2,1,0:T(8,128)(2,1)S(1)} %fusion.15), channel_id=1, source_target_pairs={{4,0},{8,4},{12,8},{16,12},{20,16},{24,20},{28,24},{32,28},{36,32}... | collective-permute-start | bytes 49160 | tf_op jit(solution)/shard_map/ppermute | solution.py:29
  34.3 1.2 copy-start.3
  36.1 6.7 %collective-permute-start.3 = (bf16[8,1,16,128]{3,2,1,0:T(8,128)(2,1)S(1)}, bf16[8,1,16,128]{3,2,1,0:T(8,128)(2,1)S(1)}, u32[]{:S(2)}, u32[]{:S(2)}) collective-permute-start(bf16[8,1,16,128]{3,2,1,0:T(8,128)(2,1)S(1)} %get-tuple-element.84), channel_id=1, source_target_pairs={{0,1},{1,2},{2,3},{4,5},{5,6},{6,7},{8,9},{9,10},{10,11},{12,13},{... | collective-permute-start | bytes 98312 | tf_op jit(solution)/shard_map/ppermute | solution.py:17
  39.5 4.7 %collective-permute-start.4 = (bf16[8,1,16,128]{3,2,1,0:T(8,128)(2,1)S(1)}, bf16[8,1,16,128]{3,2,1,0:T(8,128)(2,1)S(1)}, u32[]{:S(2)}, u32[]{:S(2)}) collective-permute-start(bf16[8,1,16,128]{3,2,1,0:T(8,128)(2,1)S(1)} %get-tuple-element.85), channel_id=1, source_target_pairs={{1,0},{2,1},{3,2},{5,4},{6,5},{7,6},{9,8},{10,9},{11,10},{13,12},{... | collective-permute-start | bytes 98312 | tf_op jit(solution)/shard_map/ppermute | solution.py:19
  44.2 4.4 %collective-permute-start.5 = (bf16[2,4,16,128]{3,2,1,0:T(8,128)(2,1)S(1)}, bf16[2,4,16,128]{3,2,1,0:T(8,128)(2,1)S(1)}, u32[]{:S(2)}, u32[]{:S(2)}) collective-permute-start(bf16[2,4,16,128]{3,2,1,0:T(8,128)(2,1)S(1)} %pad_maximum_fusion.4), channel_id=1, source_target_pairs={{0,4},{4,8},{8,12},{12,16},{16,20},{20,24},{24,28},{28,32},{32,36}... | collective-permute-start | bytes 98312 | tf_op jit(solution)/shard_map/ppermute | solution.py:29
  48.9 0.8 copy-start.2
Sparse Core Ops, SparseCore 0:
  51.8 288.8 all-reduce.31
where the time goes:
time: 351 us; the launch traced here: 350 us
  waiting for transfers between devices  291 us (83%)
  starting transfers between devices  29.1 us (8%)
  between operations  15.8 us (5%)
  matrix products  7.3 us (2%)
  local copies, waits for them, and re-layouts  5.82 us (2%)
    psum x1, waiting for transfers between devices, per_device(): grad_one, grad_two = lax.psum((grad_one, grad_two), ('tm', 'space'))  288 us
    ppermute x5, starting transfers between devices, passed_along(): lax.ppermute(value, axis, [(source, source + steps) for source in range(i...  19.1 us
    ppermute x2, starting transfers between devices, with_halo(): lax.ppermute(tail, axis, [(i, (i + 1) % count) for i in range(ends)])  7.34 us
  transfers between devices with their start and end apart: 10, of which 4 were waited for; matrix products, arithmetic and copies ran while one was open for 2% of the time, Pallas kernels for 0%

commit v1 on v0

v1 whole, which is shorter than its diff:
```python
import math

import jax
import jax.numpy as jnp
from jax import lax
from jax.experimental import pallas as pl
from jax.experimental.pallas import tpu as pltpu
from jax.sharding import PartitionSpec as P

MESH = pl.DeviceIdType.MESH
SIDE = 8
BLOCK = 112
TILE = 16


def build_patches(extended, frames, height, columns):
    pieces = []
    for depth in range(3):
        for down in range(3):
            for across in range(3):
                pieces.append(
                    extended[
                        depth : depth + frames, down : down + height, across : across + columns, :
                    ]
                )
    stacked = jnp.concatenate(pieces, axis=-1)
    return stacked.reshape(frames * height * columns, stacked.shape[-1])


def silu_slope(value):
    sigma = jax.nn.sigmoid(value)
    return sigma * (1.0 + value * (1.0 - sigma))


def contract(patches, delta):
    return lax.dot_general(
        patches, delta, (((0,), (0,)), ((), ())), preferred_element_type=jnp.float32
    )


def passed_along(value, axis, steps):
    count = lax.axis_size(axis)
    initial, last = (max(0, -steps), min(count, count - steps))
    return lax.ppermute(value, axis, [(source, source + steps) for source in range(initial, last)])


def reduce_kernel(
    scale, part_ref, one_ref, two_ref,
    swap_out, swap_in, total, stage, land_a, stage_b, land_b, mine, tiles, wide, other,
    swap_send, swap_recv, a_send, a_recv, b_send, b_recv, tb_send, tb_recv,
    ta_send, ta_recv, o_send, o_recv,
):
    tm = lax.axis_index("tm")
    space = lax.axis_index("space")
    core = lax.rem(tm, 2)
    chip = tm // 2
    y, z = chip // SIDE, lax.rem(chip, SIDE)
    a = y * (1 - core) + z * core
    b = z * (1 - core) + y * core
    stride_a, stride_b = 8 - 7 * core, 1 + 7 * core
    rows = one_ref.shape[0]

    def along_a(step):
        at = lax.rem(a + step, SIDE)
        return at, (2 * (at * stride_a + b * stride_b) + core, space)

    def along_b(step):
        at = lax.rem(b + step, SIDE)
        return at, (2 * (a * stride_a + at * stride_b) + core, space)

    sibling = (tm + 1 - 2 * core, space)

    barrier = pltpu.get_barrier_semaphore()
    pl.semaphore_signal(barrier, inc=1, device_id=sibling, device_id_type=MESH)
    for step in range(1, SIDE):
        pl.semaphore_signal(barrier, inc=1, device_id=along_a(step)[1], device_id_type=MESH)
        pl.semaphore_signal(barrier, inc=1, device_id=along_b(step)[1], device_id_type=MESH)
    pl.semaphore_wait(barrier, 2 * SIDE - 1)

    def send(source, target, send_sem, recv_sem, device):
        copy = pltpu.make_async_remote_copy(
            src_ref=source, dst_ref=target, send_sem=send_sem, recv_sem=recv_sem,
            device_id=device, device_id_type=MESH,
        )
        copy.start()
        return copy

    swap_out[...] = part_ref[1 - core].astype(jnp.bfloat16)
    swap = send(swap_out, swap_in, swap_send, swap_recv, sibling)
    swap.wait_recv()
    total[0:rows] = part_ref[core] + swap_in[...].astype(jnp.float32)
    total[rows:] = jnp.zeros((SIDE * BLOCK - rows, total.shape[1]), jnp.float32)
    stage[...] = total[...].astype(jnp.bfloat16).reshape(stage.shape)

    over_a = []
    for step in range(1, SIDE):
        at, device = along_a(step)
        over_a.append(
            send(stage.at[at], land_a.at[step - 1], a_send.at[step - 1], a_recv.at[step - 1], device)
        )
    block = total[pl.ds(a * BLOCK, BLOCK)]
    for step in range(1, SIDE):
        over_a[step - 1].wait_recv()
        block = block + land_a[step - 1].astype(jnp.float32)
    total[0:BLOCK] = block
    total[BLOCK : BLOCK + TILE] = jnp.zeros((TILE, total.shape[1]), jnp.float32)
    stage_b[...] = total[0 : BLOCK + TILE].astype(jnp.bfloat16).reshape(stage_b.shape)

    over_b = []
    for step in range(1, SIDE):
        at, device = along_b(step)
        over_b.append(
            send(stage_b.at[at], land_b.at[step - 1], b_send.at[step - 1], b_recv.at[step - 1], device)
        )
    tile = total[pl.ds(b * TILE, TILE)]
    for step in range(1, SIDE):
        over_b[step - 1].wait_recv()
        tile = tile + land_b[step - 1].astype(jnp.float32)
    mine[...] = (tile * scale).astype(jnp.bfloat16)
    tiles[b] = mine[...]

    back_b = []
    for step in range(1, SIDE):
        at, device = along_b(step)
        back_b.append(
            send(mine, tiles.at[b], tb_send.at[step - 1], tb_recv.at[step - 1], device)
        )
    for step in range(1, SIDE):
        back_b[step - 1].wait_recv()
    wide[a] = tiles[0 : SIDE - 1].reshape(BLOCK, tiles.shape[-1])

    back_a = []
    for step in range(1, SIDE):
        at, device = along_a(step)
        back_a.append(
            send(wide.at[a], wide.at[a], ta_send.at[step - 1], ta_recv.at[step - 1], device)
        )
    across = [send(wide.at[a], other.at[a], o_send.at[0], o_recv.at[0], sibling)]
    for step in range(1, SIDE):
        back_a[step - 1].wait_recv()
        origin = lax.rem(a + SIDE - step, SIDE)
        across.append(
            send(wide.at[origin], other.at[origin], o_send.at[step], o_recv.at[step], sibling)
        )
    for copy in across:
        copy.wait_recv()
    full = wide[...].astype(jnp.float32).reshape(SIDE * BLOCK, -1)[0:rows]
    rest = other[...].astype(jnp.float32).reshape(SIDE * BLOCK, -1)[0:rows]
    one_ref[...] = jnp.where(core == 0, full, rest)
    two_ref[...] = jnp.where(core == 0, rest, full)
    for copy in [swap] + over_a + over_b + back_b + back_a + across:
        copy.wait_send()


def reduced(part, scale):
    rows, width = part.shape[1:]
    half = jnp.bfloat16
    full = jnp.float32
    dma = pltpu.SemaphoreType.DMA
    return pl.pallas_call(
        lambda *refs: reduce_kernel(scale, *refs),
        out_shape=(jax.ShapeDtypeStruct((rows, width), full),) * 2,
        in_specs=[pl.BlockSpec(memory_space=pltpu.VMEM)],
        out_specs=(pl.BlockSpec(memory_space=pltpu.VMEM),) * 2,
        scratch_shapes=[
            pltpu.VMEM((rows, width), half),
            pltpu.VMEM((rows, width), half),
            pltpu.VMEM((SIDE * BLOCK, width), full),
            pltpu.VMEM((SIDE, BLOCK, width), half),
            pltpu.VMEM((SIDE - 1, BLOCK, width), half),
            pltpu.VMEM((SIDE, TILE, width), half),
            pltpu.VMEM((SIDE - 1, TILE, width), half),
            pltpu.VMEM((TILE, width), half),
            pltpu.VMEM((SIDE, TILE, width), half),
            pltpu.VMEM((SIDE, BLOCK, width), half),
            pltpu.VMEM((SIDE, BLOCK, width), half),
            dma,
            dma,
            dma((SIDE - 1,)),
            dma((SIDE - 1,)),
            dma((SIDE - 1,)),
            dma((SIDE - 1,)),
            dma((SIDE - 1,)),
            dma((SIDE - 1,)),
            dma((SIDE - 1,)),
            dma((SIDE - 1,)),
            dma((SIDE,)),
            dma((SIDE,)),
        ],
        compiler_params=pltpu.CompilerParams(
            collective_id=0, has_side_effects=True, vmem_limit_bytes=32 * 1024 * 1024
        ),
    )(part)


def extend(field, starting):
    earlier = passed_along(field[field.shape[0] - 2 :], "tm", 1)
    own_first = jnp.concatenate([field[:1], field[:1]], axis=0)
    cache = jnp.where(starting, own_first, earlier)
    joined = jnp.concatenate([cache, field], axis=0)
    return jnp.pad(joined, ((0, 0), (1, 1), (1, 1), (0, 0)))


def per_device(video, cotangent, weight_one, weight_two, predecessor, frame_count):
    space = lax.axis_index("space")
    low = video.shape[2]
    both = lax.all_gather(jnp.concatenate([video, cotangent]), "space", axis=2, tiled=True)
    field, change = both[0], both[1]
    frames, height, columns, width = field.shape
    starting = predecessor[0] < 0
    live = (jnp.arange(frames) < frame_count[0]).astype(jnp.float32)[:, None, None, None]
    scale = 1.0 / math.sqrt(lax.axis_size("tm") * frames * height * columns)
    patches_one = build_patches(extend(field, starting), frames, height, columns)
    first_act = jnp.dot(patches_one, weight_one, preferred_element_type=jnp.float32).reshape(
        frames, height, columns, width
    )
    hidden = (live * jax.nn.silu(first_act)).astype(jnp.bfloat16)
    ext_two = extend(hidden, starting)
    patches_two = build_patches(ext_two, frames, height, columns)
    near = lax.dynamic_slice_in_dim(ext_two, space * low, low + 2, 1)
    second_act = jnp.dot(
        build_patches(near, frames, low, columns), weight_two, preferred_element_type=jnp.float32
    ).reshape(frames, low, columns, width)
    output = (live * (video[0].astype(jnp.float32) + second_act)).astype(jnp.bfloat16)
    delta_two = (live * change.astype(jnp.float32)).astype(jnp.bfloat16).reshape(-1, width)
    back = lax.dot_general(
        delta_two, weight_two, (((1,), (1,)), ((), ())), preferred_element_type=jnp.float32
    )
    _, pull = jax.vjp(
        lambda grid: build_patches(grid, frames, height, columns),
        jnp.zeros(ext_two.shape, jnp.float32),
    )
    spread = pull(back)[0][:, 1 : height + 1, 1 : columns + 1]
    cache_part = spread[:2]
    own = spread[2:]
    passing = jnp.where(starting, 0.0, cache_part)
    from_next = passed_along(passing.astype(jnp.bfloat16), "tm", -1).astype(passing.dtype)
    own = own.at[frames - 2 :].add(from_next)
    own = own.at[0].add(jnp.where(starting, cache_part[0] + cache_part[1], 0.0))
    delta_one = (own * live * silu_slope(first_act)).astype(jnp.bfloat16).reshape(-1, width)
    count = patches_one.shape[1] // lax.axis_size("space")
    share_one = lax.dynamic_slice_in_dim(patches_one, space * count, count, 1)
    share_two = lax.dynamic_slice_in_dim(patches_two, space * count, count, 1)
    part = jnp.stack([contract(share_one, delta_one), contract(share_two, delta_two)])
    grad_one, grad_two = reduced(part, scale)
    return (output[None], grad_one, grad_two)


def solution(mesh):
    placed = (
        P("tm", None, "space", None, None),
        P("tm", None, "space", None, None),
        P(),
        P(),
        P("tm"),
        P("tm"),
    )
    return jax.shard_map(
        per_device,
        mesh=mesh,
        in_specs=placed,
        out_specs=(P("tm", None, "space", None, None), P("space", None), P("space", None)),
        check_vma=False,
    )
```

time: 351 us -> 107 us (0.30)
  waiting for transfers between devices: 291 us -> 0.01 us
  Pallas kernels: 0 us -> 40.1 us
  starting transfers between devices: 29.1 us -> 14.7 us
  local copies, waits for them, and re-layouts: 5.82 us -> 18.9 us
  between operations: 15.8 us -> 3.38 us
  blocking collectives: 0 us -> 11.1 us
  other arithmetic: 0.68 us -> 10.1 us
    psum x1 -> x0, waiting for transfers between devices: 288 us -> none  [per_device(): grad_one, grad_two = lax.psum((grad_one, grad_two), ('tm', 'space'))]
    pallas_call x0 -> x1, Pallas kernels: none -> 40.1 us  [reduced(): pl.pallas_call(lambda *refs: reduce_kernel(scale, *refs), out_shape=(jax....]
    all_gather x0 -> x1, blocking collectives: none -> 11.1 us  [per_device(): lax.all_gather(jnp.concatenate([video, cotangent]), 'space', axis=2, tile...]
    ppermute x4 -> x0, starting transfers between devices: 9.92 us -> none  [the longest x2 7.34 us: with_halo(): lax.ppermute(tail, axis, [(i, (i + 1) % count) for i in range(ends)])]
    unnamed x56 -> x139, local copies, waits for them, and re-layouts: 2.25 us -> 10.9 us
    add_any x0 -> x1, other arithmetic: none -> 4.79 us  [build_patches(): extended[depth:depth + frames, down:down + height, across:across + column...]
    ppermute x5 -> x3, starting transfers between devices: 19.1 us -> 14.7 us  [passed_along(): lax.ppermute(value, axis, [(source, source + steps) for source in range(i...]
    split x2, local copies, waits for them, and re-layouts: 0.47 us -> 4.16 us  [build_patches(): stacked = jnp.concatenate(pieces, axis=-1)]
  transfers between devices with their start and end apart: 10 -> 3, of which waited for: 4 -> 0; matrix products, arithmetic and copies ran while one was open for 2% -> 7% of each run, Pallas kernels for 0% -> 0%
where the time goes in v1:
time: 107 us; the launch traced here: 106 us
  Pallas kernels  40.1 us (37%)
  local copies, waits for them, and re-layouts  18.9 us (18%)
  starting transfers between devices  14.7 us (14%)
  blocking collectives  11.1 us (10%)
  other arithmetic  10.1 us (9%)
  matrix products  8.09 us (8%)
  between operations  3.38 us (3%)
    pallas_call x1, Pallas kernels, reduced(): pl.pallas_call(lambda *refs: reduce_kernel(scale, *refs), out_shape=(jax....  40.1 us
    ppermute x3, starting transfers between devices, passed_along(): lax.ppermute(value, axis, [(source, source + steps) for source in range(i...  14.7 us
    all_gather x1, blocking collectives, per_device(): lax.all_gather(jnp.concatenate([video, cotangent]), 'space', axis=2, tile...  11.1 us
    unnamed x139, local copies, waits for them, and re-layouts  10.9 us
    add_any x1, other arithmetic, build_patches(): extended[depth:depth + frames, down:down + height, across:across + column...  4.79 us
    split x2, local copies, waits for them, and re-layouts, build_patches(): stacked = jnp.concatenate(pieces, axis=-1)  4.16 us
    dot_general x2, matrix products, contract(): lax.dot_general(patches, delta, (((0,), (0,)), ((), ())), preferred_eleme...  2.63 us
    dot_general x1, matrix products, per_device(): jnp.dot(patches_one, weight_one, preferred_element_type=jnp.float32)  2.15 us
  transfers between devices with their start and end apart: 3, of which 0 were waited for; matrix products, arithmetic and copies ran while one was open for 7% of the time, Pallas kernels for 0%

profile of v1, /device:TPU:1, one launch (start us, length us, event | category | flops | bytes accessed | tf_op | source)
XLA Modules:
  0.0 106.4 jit_solution(17464430704871432702)
XLA Ops:
  1.4 0.9 pad_maximum_fusion.3
  2.3 11.1 %all_gather.3 = bf16[2,8,8,16,128]{4,3,2,1,0:T(8,128)(2,1)S(1)} all-gather(bf16[2,8,2,16,128]{4,3,2,1,0:T(8,128)(2,1)S(1)} %pad_maximum_fusion.3), channel_id=1, replica_groups=mesh['tm'=128,'space'=4] {'space'}, dimensions={2}, use_global_device_ids=true | all-gather | bytes 655360 | tf_op jit(solution)/shard_map/all_gather | solution.py:207
  13.4 2.1 %fusion.15 = f32[8,8,16,3456]{3,2,1,0:T(8,128)S(1)} fusion(bf16[3456,128]{1,0:T(8,128)(2,1)S(1)} %copy-done, f32[8]{0:T(128)S(1)} %compare_convert_fusion, bf16[2,8,8,16,128]{4,3,2,1,0:T(8,128)(2,1)S(1)} %all_gather.3), kind=kOutput, calls=%fused_computation.89 | convolution fusion | flops 906362880 | bytes 15303168 | tf_op jit(solution)/shard_map/dot_general | solution.py:226
  15.4 3.6 %fusion.61 = (f32[8,8,16,128]{3,2,1,0:T(8,128)S(1)}, f32[8,8,16,128]{3,2,1,0:T(8,128)}, f32[8,8,16,128]{3,2,1,0:T(8,128)}, f32[8,8,16,128]{3,2,1,0:T(8,128)}, f3...) fusion(f32[8,8,16,3456]{3,2,1,0:T(8,128)S(1)} %fusion.15), kind=kLoop, calls=%fused_computation.240 | loop fusion | bytes 19922944 | tf_op jit(solution)/shard_map/transpose(jvp())/split | solution.py:26
  19.2 0.5 fusion.62
  20.9 0.2 copy-done.7
  21.0 0.2 copy-done.8
  21.2 0.2 copy-done.9
  21.3 0.2 copy-done.10
  21.5 0.2 copy-done.11
  21.7 0.2 copy-done.12
  21.8 0.2 copy-done.13
  22.0 0.2 copy-done.14
  22.4 4.8 %pad_add_fusion = f32[10,10,18,128]{3,2,1,0:T(8,128)} fusion(f32[8,8,16,128]{3,2,1,0:T(8,128)S(1)} %copy-done.1, f32[8,8,16,128]{3,2,1,0:T(8,128)S(1)} %copy-done.2, f32[8,8,16,128]{3,2,1,0:T(8,128)S(1)} %copy-done.3, f32[8,8,16,128]{3,2,1,0:T(8,128)S(1)} %copy-done.4, f32[8,8,16,128]{3,2,1,0:T(8,128)S(1)} %copy-done.5, f32[8,8,16,128]{3,2,1,0:T(8,128)S(1)} %copy-done.6, ...), kind=kLoop, calls=%fused_computation.79 | loop fusion | flops 5990400 | bytes 15077376 | tf_op jit(solution)/shard_map/transpose(jvp())/add_any | solution.py:22
  27.2 1.6 %fusion.52 = bf16[2,8,16,128]{3,2,1,0:T(8,128)(2,1)} fusion(f32[10,10,18,128]{3,2,1,0:T(8,128)} %pad_add_fusion, pred[]{:T(512)} %bitcast.2), kind=kLoop, calls=%fused_computation.224 | loop fusion | flops 32768 | bytes 131073 | tf_op jit(solution)/shard_map/convert_element_type | solution.py:237
  28.8 10.5 %collective-permute-start.2 = (bf16[2,8,16,128]{3,2,1,0:T(8,128)(2,1)}, bf16[2,8,16,128]{3,2,1,0:T(8,128)(2,1)S(1)}, u32[]{:S(2)}, u32[]{:S(2)}) collective-permute-start(bf16[2,8,16,128]{3,2,1,0:T(8,128)(2,1)} %fusion.52), channel_id=1, source_target_pairs={{4,0},{8,4},{12,8},{16,12},{20,16},{24,20},{28,24},{32,28},{36,32}... | collective-permute-start | bytes 196616 | tf_op jit(solution)/shard_map/ppermute | solution.py:44
  39.3 0.6 slice_bitcast_fusion
  39.9 1.9 %collective-permute-start = (bf16[2,8,16,128]{3,2,1,0:T(8,128)(2,1)}, bf16[2,8,16,128]{3,2,1,0:T(8,128)(2,1)S(1)}, u32[]{:S(2)}, u32[]{:S(2)}) collective-permute-start(bf16[2,8,16,128]{3,2,1,0:T(8,128)(2,1)} %slice_bitcast_fusion), channel_id=1, source_target_pairs={{0,4},{4,8},{8,12},{12,16},{16,20},{20,24},{24,28},{28,32},{32,36}... | collective-permute-start | bytes 196616 | tf_op jit(solution)/shard_map/ppermute | solution.py:44
  42.2 0.2 fusion.18
  42.4 1.2 %slice.450 = f32[8,8,16,128]{3,2,1,0:T(8,128)S(1)} slice(f32[10,10,18,128]{3,2,1,0:T(8,128)} %pad_add_fusion), slice={[2:10], [1:9], [1:17], [0:128]} | slice | bytes 1048576 | tf_op jit(solution)/shard_map/slice | solution.py:235
  43.6 1.0 fusion.53
  44.6 1.0 fusion.56
  48.3 0.4 pad_slice_fusion.25
  48.8 1.1 %pad_slice_fusion.24 = (bf16[8,8,16,128]{3,2,1,0:T(8,128)(2,1)S(1)}, bf16[8,8,16,3456]{3,2,1,0:T(8,128)(2,1)S(1)}, bf16[8,8,16,128]{3,2,1,0:T(8,128)(2,1)S(1)}, ...) fusion(bf16[10,8,16,128]{3,2,1,0:T(8,128)(2,1)S(1)} %pad_maximu, ...), kind=kLoop, calls=%fused_computation.51 | loop fusion | bytes 5046272 | tf_op jit(solution)/shard_map/slice | solution.py:22
  49.9 2.2 %multiply_convert_fusion = (bf16[8,8,16,128]{3,2,1,0:T(8,128)(2,1)S(1)}, bf16[8,8,16,128]{3,2,1,0:T(8,128)(2,1)S(1)}) fusion(f32[8,8,16,128]{3,2,1,0:T(8,128)S(1)} %fusion.56, f32[8]{0:T(128)S(1)} %compare_convert_fusion, bf16[8,8,16,3456]{3,2,1,0:T(8,128)(2,1)S(1)} %get-tuple-element.68, bf16[3456,128]{1,0:T(8,128)(2,1)S(1)} %copy-done.18), kind=kOutput, calls=%fused_computation.96 | convolution fusion | flops 907673600 | bytes 9011232 | tf_op jit(solution)/shard_map/dot_general | solution.py:214
  52.1 2.3 %collective-permute-start.1 = (bf16[2,8,16,128]{3,2,1,0:T(8,128)(2,1)S(1)}, bf16[2,8,16,128]{3,2,1,0:T(8,128)(2,1)S(1)}, u32[]{:S(2)}, u32[]{:S(2)}) collective-permute-start(bf16[2,8,16,128]{3,2,1,0:T(8,128)(2,1)S(1)} %slice.448), channel_id=1, source_target_pairs={{0,4},{4,8},{8,12},{12,16},{16,20},{20,24},{24,28},{28,32},{32,36}... | collective-permute-start | bytes 196616 | tf_op jit(solution)/shard_map/ppermute | solution.py:44
  56.3 1.3 %fusion.4 = f32[1,864,128]{2,1,0:T(8,128)S(1)} fusion(bf16[1024,128]{1,0:T(8,128)(2,1)S(1)} %bitcast.103, bf16[1024,3456]{1,0:T(8,128)(2,1)S(1)} %constant_dynamic-update-slice_fusion.54, s32[]{:T(128)S(6)} %select_n.38), kind=kOutput, calls=%fused_computation.80 | convolution fusion | flops 226492416 | bytes 2539524 | tf_op jit(solution)/shard_map/dot_general | solution.py:36
  59.4 1.3 %fusion.12 = bf16[1,8,2,16,128]{4,3,2,1,0:T(8,128)(2,1)} fusion(bf16[8,2,16,3456]{3,2,1,0:T(8,128)(2,1)S(1)} %constant_dynamic-update-slice_fusion.27, bf16[3456,128]{1,0:T(8,128)(2,1)S(1)} %copy-done, bf16[1,8,2,16,128]{4,3,2,1,0:T(8,128)(2,1)S(1)} %copy-done.17, f32[8]{0:T(128)S(1)} %compare_convert_fusion), kind=kOutput, calls=%fused_computation.85 | convolution fusion | flops 226623488 | bytes 2785312 | tf_op jit(solution)/shard_map/dot_general | solution.py:221
  63.3 1.3 %fusion.7 = f32[1,864,128]{2,1,0:T(8,128)S(1)} fusion(bf16[1024,128]{1,0:T(8,128)(2,1)S(1)} %fusion.18, bf16[1024,3456]{1,0:T(8,128)(2,1)S(1)} %bitcast.102, s32[]{:T(128)S(6)} %select_n.38), kind=kOutput, calls=%fused_computation.81 | convolution fusion | flops 226492416 | bytes 2539524 | tf_op jit(solution)/shard_map/dot_general | solution.py:36
  64.7 40.1 %shard_map.85 = (f32[864,128]{1,0:T(8,128)S(1)}, f32[864,128]{1,0:T(8,128)S(1)}) custom-call(f32[2,864,128]{2,1,0:T(8,128)S(1)} %pad_maximum_fusion.refs_0_), custom_call_target="tpu_custom_call" | custom-call | tf_op jit(solution)/shard_map/pallas_call | solution.py:160
  104.8 0.8 copy.121
  105.6 0.8 copy.122
  (151 shorter events, 9.3 us)
Async XLA Ops:
  0.6 12.7 %copy-start = (bf16[3456,128]{1,0:T(8,128)(2,1)S(1)}, bf16[3456,128]{1,0:T(8,128)(2,1)}, u32[]{:S(2)}) copy-start(bf16[3456,128]{1,0:T(8,128)(2,1)} %param.13) | copy-start | bytes 2654212
  19.0 1.7 %copy-start.1 = (f32[8,8,16,128]{3,2,1,0:T(8,128)S(1)}, f32[8,8,16,128]{3,2,1,0:T(8,128)}, u32[]{:S(2)}) copy-start(f32[8,8,16,128]{3,2,1,0:T(8,128)} %get-tuple-element.36) | copy-start | bytes 1572868
  19.0 1.7 %copy-start.2 = (f32[8,8,16,128]{3,2,1,0:T(8,128)S(1)}, f32[8,8,16,128]{3,2,1,0:T(8,128)}, u32[]{:S(2)}) copy-start(f32[8,8,16,128]{3,2,1,0:T(8,128)} %get-tuple-element.37) | copy-start | bytes 1572868
  19.0 1.7 %copy-start.3 = (f32[8,8,16,128]{3,2,1,0:T(8,128)S(1)}, f32[8,8,16,128]{3,2,1,0:T(8,128)}, u32[]{:S(2)}) copy-start(f32[8,8,16,128]{3,2,1,0:T(8,128)} %get-tuple-element.38) | copy-start | bytes 1572868
  19.0 1.7 %copy-start.4 = (f32[8,8,16,128]{3,2,1,0:T(8,128)S(1)}, f32[8,8,16,128]{3,2,1,0:T(8,128)}, u32[]{:S(2)}) copy-start(f32[8,8,16,128]{3,2,1,0:T(8,128)} %get-tuple-element.39) | copy-start | bytes 1572868
  19.1 1.7 %copy-start.5 = (f32[8,8,16,128]{3,2,1,0:T(8,128)S(1)}, f32[8,8,16,128]{3,2,1,0:T(8,128)}, u32[]{:S(2)}) copy-start(f32[8,8,16,128]{3,2,1,0:T(8,128)} %get-tuple-element.40) | copy-start | bytes 1572868
  19.1 1.8 %copy-start.6 = (f32[8,8,16,128]{3,2,1,0:T(8,128)S(1)}, f32[8,8,16,128]{3,2,1,0:T(8,128)}, u32[]{:S(2)}) copy-start(f32[8,8,16,128]{3,2,1,0:T(8,128)} %get-tuple-element.41) | copy-start | bytes 1572868
  19.1 2.0 %copy-start.7 = (f32[8,8,16,128]{3,2,1,0:T(8,128)S(1)}, f32[8,8,16,128]{3,2,1,0:T(8,128)}, u32[]{:S(2)}) copy-start(f32[8,8,16,128]{3,2,1,0:T(8,128)} %get-tuple-element.42) | copy-start | bytes 1572868
  19.1 2.1 %copy-start.8 = (f32[8,8,16,128]{3,2,1,0:T(8,128)S(1)}, f32[8,8,16,128]{3,2,1,0:T(8,128)}, u32[]{:S(2)}) copy-start(f32[8,8,16,128]{3,2,1,0:T(8,128)} %get-tuple-element.43) | copy-start | bytes 1572868
  19.1 2.3 %copy-start.9 = (f32[8,8,16,128]{3,2,1,0:T(8,128)S(1)}, f32[8,8,16,128]{3,2,1,0:T(8,128)}, u32[]{:S(2)}) copy-start(f32[8,8,16,128]{3,2,1,0:T(8,128)} %get-tuple-element.44) | copy-start | bytes 1572868
  19.1 2.4 %copy-start.10 = (f32[8,8,16,128]{3,2,1,0:T(8,128)S(1)}, f32[8,8,16,128]{3,2,1,0:T(8,128)}, u32[]{:S(2)}) copy-start(f32[8,8,16,128]{3,2,1,0:T(8,128)} %get-tuple-element.45) | copy-start | bytes 1572868
  19.1 2.6 %copy-start.11 = (f32[8,8,16,128]{3,2,1,0:T(8,128)S(1)}, f32[8,8,16,128]{3,2,1,0:T(8,128)}, u32[]{:S(2)}) copy-start(f32[8,8,16,128]{3,2,1,0:T(8,128)} %get-tuple-element.46) | copy-start | bytes 1572868
  19.1 2.7 %copy-start.12 = (f32[8,8,16,128]{3,2,1,0:T(8,128)S(1)}, f32[8,8,16,128]{3,2,1,0:T(8,128)}, u32[]{:S(2)}) copy-start(f32[8,8,16,128]{3,2,1,0:T(8,128)} %get-tuple-element.47) | copy-start | bytes 1572868
  19.1 2.8 %copy-start.13 = (f32[8,8,16,128]{3,2,1,0:T(8,128)S(1)}, f32[8,8,16,128]{3,2,1,0:T(8,128)}, u32[]{:S(2)}) copy-start(f32[8,8,16,128]{3,2,1,0:T(8,128)} %get-tuple-element.48) | copy-start | bytes 1572868
  19.1 3.0 %copy-start.14 = (f32[8,8,16,128]{3,2,1,0:T(8,128)S(1)}, f32[8,8,16,128]{3,2,1,0:T(8,128)}, u32[]{:S(2)}) copy-start(f32[8,8,16,128]{3,2,1,0:T(8,128)} %get-tuple-element.49) | copy-start | bytes 1572868
  19.2 3.1 %copy-start.15 = (f32[8,8,16,128]{3,2,1,0:T(8,128)S(1)}, f32[8,8,16,128]{3,2,1,0:T(8,128)}, u32[]{:S(2)}) copy-start(f32[8,8,16,128]{3,2,1,0:T(8,128)} %get-tuple-element.50) | copy-start | bytes 1572868
  19.2 3.3 %copy-start.16 = (f32[8,8,16,128]{3,2,1,0:T(8,128)S(1)}, f32[8,8,16,128]{3,2,1,0:T(8,128)}, u32[]{:S(2)}) copy-start(f32[8,8,16,128]{3,2,1,0:T(8,128)} %get-tuple-element.51) | copy-start | bytes 1572868
  28.8 14.8 %collective-permute-start.2 = (bf16[2,8,16,128]{3,2,1,0:T(8,128)(2,1)}, bf16[2,8,16,128]{3,2,1,0:T(8,128)(2,1)S(1)}, u32[]{:S(2)}, u32[]{:S(2)}) collective-permute-start(bf16[2,8,16,128]{3,2,1,0:T(8,128)(2,1)} %fusion.52), channel_id=1, source_target_pairs={{4,0},{8,4},{12,8},{16,12},{20,16},{24,20},{28,24},{32,28},{36,32}... | collective-permute-start | bytes 196616 | tf_op jit(solution)/shard_map/ppermute | solution.py:44
  39.9 5.6 %collective-permute-start = (bf16[2,8,16,128]{3,2,1,0:T(8,128)(2,1)}, bf16[2,8,16,128]{3,2,1,0:T(8,128)(2,1)S(1)}, u32[]{:S(2)}, u32[]{:S(2)}) collective-permute-start(bf16[2,8,16,128]{3,2,1,0:T(8,128)(2,1)} %slice_bitcast_fusion), channel_id=1, source_target_pairs={{0,4},{4,8},{8,12},{12,16},{16,20},{20,24},{24,28},{28,32},{32,36}... | collective-permute-start | bytes 196616 | tf_op jit(solution)/shard_map/ppermute | solution.py:44
  47.2 2.8 %copy-start.18 = (bf16[3456,128]{1,0:T(8,128)(2,1)S(1)}, bf16[3456,128]{1,0:T(8,128)(2,1)}, u32[]{:S(2)}) copy-start(bf16[3456,128]{1,0:T(8,128)(2,1)} %param.12) | copy-start | bytes 2654212
  52.1 5.5 %collective-permute-start.1 = (bf16[2,8,16,128]{3,2,1,0:T(8,128)(2,1)S(1)}, bf16[2,8,16,128]{3,2,1,0:T(8,128)(2,1)S(1)}, u32[]{:S(2)}, u32[]{:S(2)}) collective-permute-start(bf16[2,8,16,128]{3,2,1,0:T(8,128)(2,1)S(1)} %slice.448), channel_id=1, source_target_pairs={{0,4},{4,8},{8,12},{12,16},{16,20},{20,24},{24,28},{28,32},{32,36}... | collective-permute-start | bytes 196616 | tf_op jit(solution)/shard_map/ppermute | solution.py:44
  56.3 3.1 %copy-start.17 = (bf16[1,8,2,16,128]{4,3,2,1,0:T(8,128)(2,1)S(1)}, bf16[1,8,2,16,128]{4,3,2,1,0:T(8,128)(2,1)}, u32[]{:S(2)}) copy-start(bf16[1,8,2,16,128]{4,3,2,1,0:T(8,128)(2,1)} %param.10) | copy-start | bytes 196612

commit v2 on v1

v2 whole, which is shorter than its diff:
```python
import math

import jax
import jax.numpy as jnp
from jax import lax
from jax.experimental import pallas as pl
from jax.experimental.pallas import tpu as pltpu
from jax.sharding import PartitionSpec as P

MESH = pl.DeviceIdType.MESH
HALF = jnp.bfloat16
FULL = jnp.float32
SIDE = 8
SPACE = 4
BLOCK = 112
FRAMES = 8
ROWS = 8
LOW = 2
COLS = 16
WIDTH = 128
PLANE = ROWS * COLS
SHARE = 864


def shifted(value, step):
    rows = value.shape[0]
    column = lax.rem(lax.broadcasted_iota(jnp.int32, value.shape, 0), COLS)
    edge = 0 if step == 1 else COLS - 1
    return jnp.where(column == edge, 0.0, pltpu.roll(value, step % rows, 0))


def joined(wide):
    left, middle, right = wide[:, :WIDTH], wide[:, WIDTH : 2 * WIDTH], wide[:, 2 * WIDTH :]
    return middle + shifted(left, 1) + shifted(right, -1)


def windows(ref, frames, start, height):
    return jnp.concatenate(
        [
            ref[kt : kt + frames, pl.ds(start + kh, height)].reshape(-1, WIDTH)
            for kt in range(3)
            for kh in range(3)
        ],
        axis=1,
    )


def forward_weight(ref):
    return jnp.concatenate(
        [
            jnp.concatenate(
                [ref[(3 * k + kw) * WIDTH : (3 * k + kw + 1) * WIDTH] for k in range(9)], axis=0
            )
            for kw in range(3)
        ],
        axis=1,
    )


def backward_weight(ref):
    return jnp.concatenate(
        [
            jnp.concatenate(
                [
                    ref[(26 - 3 * k - kw) * WIDTH : (27 - 3 * k - kw) * WIDTH]
                    for k in range(9)
                ],
                axis=1,
            )
            for kw in range(3)
        ],
        axis=0,
    )


def kernel(
    scale, video_ref, cotangent_ref, weight_one_ref, weight_two_ref, before_ref, count_ref,
    output_ref, one_ref, two_ref,
    first, second, ext_video, ext_delta, ext_hidden, cache, own_delta, next_delta, act, deltas,
    part, swap_out, swap_in, total, stage, land_a, land_b, wide, other,
    load, v_send, v_recv, vh_send, vh_recv, d_send, d_recv, dh_send, dh_recv, h_send, h_recv,
    swap_send, swap_recv, a_send, a_recv, b_send, b_recv, w_send, w_recv, o_send, o_recv,
):
    tm = lax.axis_index("tm")
    space = lax.axis_index("space")
    groups = 2 * SIDE * SIDE
    core = lax.rem(tm, 2)
    chip = tm // 2
    y, z = chip // SIDE, lax.rem(chip, SIDE)
    a = y * (1 - core) + z * core
    b = z * (1 - core) + y * core
    stride_a, stride_b = 8 - 7 * core, 1 + 7 * core

    def along_a(step):
        at = lax.rem(a + step, SIDE)
        return at, (2 * (at * stride_a + b * stride_b) + core, space)

    def along_b(step):
        at = lax.rem(b + step, SIDE)
        return at, (2 * (a * stride_a + at * stride_b) + core, space)

    def beside(step):
        return (tm, lax.rem(space + step, SPACE))

    def later(step):
        return (lax.rem(tm + 1, groups), lax.rem(space + step, SPACE))

    def earlier(step):
        return (lax.rem(tm + groups - 1, groups), lax.rem(space + step, SPACE))

    sibling = (tm + 1 - 2 * core, space)

    barrier = pltpu.get_barrier_semaphore()
    peers = [beside(step) for step in range(1, SPACE)]
    peers += [later(step) for step in range(SPACE)] + [earlier(step) for step in range(SPACE)]
    peers += [along_a(step)[1] for step in range(1, SIDE)]
    peers += [along_b(step)[1] for step in range(1, SIDE)]
    for device in peers:
        pl.semaphore_signal(barrier, inc=1, device_id=device, device_id_type=MESH)

    loads = [
        pltpu.make_async_copy(weight_one_ref, first, load.at[0]),
        pltpu.make_async_copy(weight_two_ref, second, load.at[1]),
    ]
    for copy in loads:
        copy.start()
    starting = before_ref[0] < 0
    live = [jnp.where(count_ref[0] > frame, 1.0, 0.0) for frame in range(FRAMES)]
    going = jnp.where(starting, 0.0, 1.0)
    for frame in range(FRAMES):
        masked = (live[frame] * cotangent_ref[0, frame].astype(FULL)).astype(HALF)
        own_delta[frame] = masked
        ext_delta[2 + frame, pl.ds(1 + LOW * space, LOW)] = masked
        if frame < 2:
            next_delta[frame] = (going * masked.astype(FULL)).astype(HALF)
    blank = jnp.zeros((COLS, WIDTH), HALF)
    for ref, frames in ((ext_video, 10), (ext_delta, 12), (ext_hidden, 10)):
        for frame in range(frames):
            ref[frame, 0] = blank
            ref[frame, ROWS + 1] = blank
    ext_delta[0:2] = jnp.zeros((2, ROWS + 2, COLS, WIDTH), HALF)
    ext_video[2:, pl.ds(1 + LOW * space, LOW)] = video_ref[0]
    pl.semaphore_wait(barrier, len(peers))

    sent = []

    def send(source, target, send_sem, recv_sem, device):
        copy = pltpu.make_async_remote_copy(
            src_ref=source, dst_ref=target, send_sem=send_sem, recv_sem=recv_sem,
            device_id=device, device_id_type=MESH,
        )
        copy.start()
        sent.append(copy)
        return copy

    place = pl.ds(1 + LOW * space, LOW)
    videos = [
        send(
            video_ref.at[0], ext_video.at[pl.ds(2, FRAMES), place],
            v_send.at[step - 1], v_recv.at[step - 1], beside(step),
        )
        for step in range(1, SPACE)
    ]
    videos += [
        send(
            video_ref.at[0, pl.ds(FRAMES - 2, 2)], ext_video.at[pl.ds(0, 2), place],
            vh_send.at[step], vh_recv.at[step], later(step),
        )
        for step in range(SPACE)
    ]
    changes = [
        send(
            own_delta, ext_delta.at[pl.ds(2, FRAMES), place],
            d_send.at[step - 1], d_recv.at[step - 1], beside(step),
        )
        for step in range(1, SPACE)
    ]
    changes += [
        send(
            next_delta, ext_delta.at[pl.ds(2 + FRAMES, 2), place],
            dh_send.at[step], dh_recv.at[step], earlier(step),
        )
        for step in range(SPACE)
    ]
    for copy in loads:
        copy.wait()
    for copy in videos:
        copy.wait_recv()
    for frame in range(2):
        ext_video[frame] = jnp.where(starting, ext_video[2], ext_video[frame])

    act[...] = joined(
        jnp.dot(
            windows(ext_video, FRAMES, 0, ROWS), forward_weight(first),
            preferred_element_type=FULL,
        )
    )
    for frame in range(FRAMES):
        value = act[frame * PLANE : (frame + 1) * PLANE]
        hidden = (live[frame] * (value * jax.nn.sigmoid(value))).astype(HALF)
        ext_hidden[2 + frame, 1 : 1 + ROWS] = hidden.reshape(ROWS, COLS, WIDTH)
    passing = send(
        ext_hidden.at[pl.ds(FRAMES, 2), pl.ds(1, ROWS)], cache, h_send, h_recv, later(0)
    )

    for copy in changes:
        copy.wait_recv()
    spread = joined(
        lax.dot_general(
            windows(ext_delta, FRAMES + 2, 0, ROWS), backward_weight(second),
            (((1,), (1,)), ((), ())), preferred_element_type=FULL,
        )
    )

    def put(slot, frame, value):
        at = slice(frame * PLANE, (frame + 1) * PLANE)
        deltas[slot, at, 0:WIDTH] = shifted(value, -1).astype(HALF)
        deltas[slot, at, WIDTH : 2 * WIDTH] = value.astype(HALF)
        deltas[slot, at, 2 * WIDTH :] = shifted(value, 1).astype(HALF)

    for frame in range(FRAMES):
        own = spread[(frame + 2) * PLANE : (frame + 3) * PLANE]
        if frame == 0:
            own = own + jnp.where(starting, spread[0:PLANE] + spread[PLANE : 2 * PLANE], 0.0)
        value = act[frame * PLANE : (frame + 1) * PLANE]
        sigma = jax.nn.sigmoid(value)
        put(0, frame, own * live[frame] * (sigma * (1.0 + value * (1.0 - sigma))))

    def gradient(slot, ref):
        pieces = []
        for step in range(3):
            pair = 2 * space + step
            pieces.append(
                ref[pl.ds(pair // 3, FRAMES), pl.ds(lax.rem(pair, 3), ROWS)].reshape(-1, WIDTH)
            )
        term = lax.dot_general(
            jnp.concatenate(pieces, axis=1), deltas[slot],
            (((0,), (0,)), ((), ())), preferred_element_type=FULL,
        )
        for step in range(3):
            for kw in range(3):
                at = (3 * step + kw) * WIDTH
                part[slot, at : at + WIDTH] = term[
                    step * WIDTH : (step + 1) * WIDTH, kw * WIDTH : (kw + 1) * WIDTH
                ]

    share = pl.ds(pl.multiple_of(96 * space, 32), SHARE)
    swap = pltpu.make_async_remote_copy(
        src_ref=swap_out, dst_ref=swap_in, send_sem=swap_send, recv_sem=swap_recv,
        device_id=sibling, device_id_type=MESH,
    )
    gradient(0, ext_video)

    @pl.when(core == 1)
    def _():
        swap_out[...] = part[0, share].astype(HALF)
        swap.start()

    for frame in range(FRAMES):
        put(1, frame, ext_delta[2 + frame, 1 : 1 + ROWS].reshape(PLANE, WIDTH).astype(FULL))
    passing.wait_recv()
    for frame in range(2):
        ext_hidden[frame, 1 : 1 + ROWS] = jnp.where(
            starting, ext_hidden[2, 1 : 1 + ROWS], cache[frame]
        )
    gradient(1, ext_hidden)

    @pl.when(core == 0)
    def _():
        swap_out[...] = part[1, share].astype(HALF)
        swap.start()

    swap.wait_recv()
    total[0:SHARE] = part[core, share] + swap_in[...].astype(FULL)
    total[SHARE:] = jnp.zeros((SIDE * BLOCK - SHARE, WIDTH), FULL)
    stage[...] = total[...].astype(HALF).reshape(stage.shape)
    over_a = []
    for step in range(1, SIDE):
        at, device = along_a(step)
        over_a.append(
            send(stage.at[at], land_a.at[step - 1], a_send.at[step - 1], a_recv.at[step - 1], device)
        )

    result = joined(
        jnp.dot(
            windows(ext_hidden, FRAMES, LOW * space, LOW), forward_weight(second),
            preferred_element_type=FULL,
        )
    ).reshape(FRAMES, LOW * COLS, WIDTH)
    for frame in range(FRAMES):
        value = video_ref[0, frame].reshape(LOW * COLS, WIDTH).astype(FULL) + result[frame]
        output_ref[0, frame] = (live[frame] * value).astype(HALF).reshape(LOW, COLS, WIDTH)

    block = total[pl.ds(pl.multiple_of(a * BLOCK, BLOCK), BLOCK)]
    for step in range(1, SIDE):
        over_a[step - 1].wait_recv()
        block = block + land_a[step - 1].astype(FULL)
    land_b[b] = block.astype(HALF)
    over_b = []
    for step in range(1, SIDE):
        over_b.append(
            send(
                land_b.at[b], land_b.at[b],
                b_send.at[step - 1], b_recv.at[step - 1], along_b(step)[1],
            )
        )
    for copy in over_b:
        copy.wait_recv()
    block = land_b[0].astype(FULL)
    for at in range(1, SIDE):
        block = block + land_b[at].astype(FULL)
    wide[a] = (block * scale).astype(HALF)
    back = []
    for step in range(1, SIDE):
        back.append(
            send(
                wide.at[a], wide.at[a],
                w_send.at[step - 1], w_recv.at[step - 1], along_a(step)[1],
            )
        )
    across = [send(wide.at[a], other.at[a], o_send.at[0], o_recv.at[0], sibling)]
    for step in range(1, SIDE):
        back[step - 1].wait_recv()
        origin = lax.rem(a + SIDE - step, SIDE)
        across.append(
            send(wide.at[origin], other.at[origin], o_send.at[step], o_recv.at[step], sibling)
        )
    for copy in across:
        copy.wait_recv()
    one_ref[...] = jnp.where(core == 0, wide[...], other[...])
    two_ref[...] = jnp.where(core == 0, other[...], wide[...])
    swap.wait_send()
    for copy in sent:
        copy.wait_send()


def per_device(video, cotangent, weight_one, weight_two, predecessor, frame_count):
    frames, height, columns, width = video.shape[1:]
    groups, parts = lax.axis_size("tm"), lax.axis_size("space")
    scale = 1.0 / math.sqrt(groups * parts * frames * height * columns)
    vmem = pl.BlockSpec(memory_space=pltpu.VMEM)
    smem = pl.BlockSpec(memory_space=pltpu.SMEM)
    anywhere = pl.BlockSpec(memory_space=pl.ANY)
    dma = pltpu.SemaphoreType.DMA
    taps = weight_one.shape[0]
    blocks = (SIDE, BLOCK, WIDTH)
    output, one, two = pl.pallas_call(
        lambda *refs: kernel(scale, *refs),
        out_shape=(
            jax.ShapeDtypeStruct(video.shape, HALF),
            jax.ShapeDtypeStruct(blocks, HALF),
            jax.ShapeDtypeStruct(blocks, HALF),
        ),
        in_specs=[vmem, vmem, anywhere, anywhere, smem, smem],
        out_specs=(vmem, vmem, vmem),
        scratch_shapes=[
            pltpu.VMEM((taps, WIDTH), HALF),
            pltpu.VMEM((taps, WIDTH), HALF),
            pltpu.VMEM((FRAMES + 2, ROWS + 2, COLS, WIDTH), HALF),
            pltpu.VMEM((FRAMES + 4, ROWS + 2, COLS, WIDTH), HALF),
            pltpu.VMEM((FRAMES + 2, ROWS + 2, COLS, WIDTH), HALF),
            pltpu.VMEM((2, ROWS, COLS, WIDTH), HALF),
            pltpu.VMEM((FRAMES, LOW, COLS, WIDTH), HALF),
            pltpu.VMEM((2, LOW, COLS, WIDTH), HALF),
            pltpu.VMEM((FRAMES * PLANE, WIDTH), FULL),
            pltpu.VMEM((2, FRAMES * PLANE, 3 * WIDTH), HALF),
            pltpu.VMEM((2, 9 * WIDTH, WIDTH), FULL),
            pltpu.VMEM((SHARE, WIDTH), HALF),
            pltpu.VMEM((SHARE, WIDTH), HALF),
            pltpu.VMEM((SIDE * BLOCK, WIDTH), FULL),
            pltpu.VMEM(blocks, HALF),
            pltpu.VMEM((SIDE - 1, BLOCK, WIDTH), HALF),
            pltpu.VMEM(blocks, HALF),
            pltpu.VMEM(blocks, HALF),
            pltpu.VMEM(blocks, HALF),
            dma((2,)),
            dma((SPACE - 1,)),
            dma((SPACE - 1,)),
            dma((SPACE,)),
            dma((SPACE,)),
            dma((SPACE - 1,)),
            dma((SPACE - 1,)),
            dma((SPACE,)),
            dma((SPACE,)),
            dma,
            dma,
            dma,
            dma,
            dma((SIDE - 1,)),
            dma((SIDE - 1,)),
            dma((SIDE - 1,)),
            dma((SIDE - 1,)),
            dma((SIDE - 1,)),
            dma((SIDE - 1,)),
            dma((SIDE,)),
            dma((SIDE,)),
        ],
        compiler_params=pltpu.CompilerParams(
            collective_id=0, has_side_effects=True, vmem_limit_bytes=48 * 1024 * 1024
        ),
    )(video, cotangent, weight_one, weight_two, predecessor, frame_count)

    def widened(grad):
        return grad.reshape(-1, WIDTH)[: taps // parts].astype(FULL)

    return (output, widened(one), widened(two))


def solution(mesh):
    placed = (
        P("tm", None, "space", None, None),
        P("tm", None, "space", None, None),
        P(),
        P(),
        P("tm"),
        P("tm"),
    )
    return jax.shard_map(
        per_device,
        mesh=mesh,
        in_specs=placed,
        out_specs=(P("tm", None, "space", None, None), P("space", None), P("space", None)),
        check_vma=False,
    )
```

time: 107 us -> 57.4 us (0.54)
  starting transfers between devices: 14.7 us -> 0 us
  local copies, waits for them, and re-layouts: 18.9 us -> 4.63 us
  blocking collectives: 11.1 us -> 0 us
  Pallas kernels: 40.1 us -> 49.6 us
  other arithmetic: 10.1 us -> 0.97 us
  matrix products: 8.09 us -> 0 us
  between operations: 3.38 us -> 1.94 us
    ppermute x3 -> x0, starting transfers between devices: 14.7 us -> none  [passed_along(): lax.ppermute(value, axis, [(source, source + steps) for source in range(i...]
    all_gather x1 -> x0, blocking collectives: 11.1 us -> none  [per_device(): lax.all_gather(jnp.concatenate([video, cotangent]), 'space', axis=2, tile...]
    pallas_call x1, Pallas kernels: 40.1 us -> 49.6 us  [per_device(): pl.pallas_call(lambda *refs: kernel(scale, *refs), out_shape=(jax.ShapeDt...]
    dot_general x5 -> x0, matrix products: 8.09 us -> none  [the longest x2 2.63 us: contract(): lax.dot_general(patches, delta, (((0,), (0,)), ((), ())), preferred_eleme...]
    unnamed x139 -> x9, local copies, waits for them, and re-layouts: 10.9 us -> 4.63 us
    add_any x1 -> x0, other arithmetic: 4.79 us -> none  [build_patches(): extended[depth:depth + frames, down:down + height, across:across + column...]
    split x2 -> x0, local copies, waits for them, and re-layouts: 4.16 us -> none  [build_patches(): stacked = jnp.concatenate(pieces, axis=-1)]
    slice x7 -> x0, local copies, waits for them, and re-layouts: 3.41 us -> none  [the longest x2 1.57 us: build_patches(): extended[depth:depth + frames, down:down + height, across:across + column...]
  transfers between devices with their start and end apart: 3 -> 0, of which waited for: 0 -> 0; matrix products, arithmetic and copies ran while one was open for 7% -> 0% of each run, Pallas kernels for 0% -> 0%
where the time goes in v2:
time: 57.4 us; the launch traced here: 57.1 us
  Pallas kernels  49.6 us (86%)
  local copies, waits for them, and re-layouts  4.63 us (8%)
  between operations  1.94 us (3%)
  other arithmetic  0.97 us (2%)
    pallas_call x1, Pallas kernels, per_device(): pl.pallas_call(lambda *refs: kernel(scale, *refs), out_shape=(jax.ShapeDt...  49.6 us
    unnamed x9, local copies, waits for them, and re-layouts  4.63 us

profile of v2, /device:TPU:1, one launch (start us, length us, event | category | flops | bytes accessed | tf_op | source)
XLA Modules:
  0.0 57.1 jit_solution(12451643014637828232)
XLA Ops:
  1.9 0.0 copy-start
  1.9 1.2 %copy-done = bf16[3456,128]{1,0:T(8,128)(2,1)S(1)} copy-done((bf16[3456,128]{1,0:T(8,128)(2,1)S(1)}, bf16[3456,128]{1,0:T(8,128)(2,1)}, u32[]{:S(2)}) %copy-start) | copy-done | bytes 884760
  3.1 0.0 copy-start.1
  3.1 1.2 %copy-done.1 = bf16[3456,128]{1,0:T(8,128)(2,1)S(1)} copy-done((bf16[3456,128]{1,0:T(8,128)(2,1)S(1)}, bf16[3456,128]{1,0:T(8,128)(2,1)}, u32[]{:S(2)}) %copy-start.1) | copy-done | bytes 884760
  4.3 0.0 copy-start.2
  4.3 0.8 %copy-done.2 = bf16[1,8,2,16,128]{4,3,2,1,0:T(8,128)(2,1)S(1)} copy-done((bf16[1,8,2,16,128]{4,3,2,1,0:T(8,128)(2,1)S(1)}, bf16[1,8,2,16,128]{4,3,2,1,0:T(8,128)(2,1)}, u32[]{:S(2)}) %copy-start.2) | copy-done | bytes 65560
  5.1 0.0 copy-start.3
  5.1 0.8 %copy-done.3 = bf16[1,8,2,16,128]{4,3,2,1,0:T(8,128)(2,1)S(1)} copy-done((bf16[1,8,2,16,128]{4,3,2,1,0:T(8,128)(2,1)S(1)}, bf16[1,8,2,16,128]{4,3,2,1,0:T(8,128)(2,1)}, u32[]{:S(2)}) %copy-start.3) | copy-done | bytes 65560
  5.9 49.6 %shard_map.85 = (bf16[1,8,2,16,128]{4,3,2,1,0:T(8,128)(2,1)S(1)}, bf16[8,112,128]{2,1,0:T(8,128)(2,1)S(1)}, bf16[8,112,128]{2,1,0:T(8,128)(2,1)S(1)}) custom-call(bf16[1,8,2,16,128]{4,3,2,1,0:T(8,128)(2,1)S(1)} %copy-done.2, bf16[1,8,2,16,128]{4,3,2,1,0:T(8,128)(2,1)S(1)} %copy-done.3, bf16[3456,128]{1,0:T(8,128)(2,1)S(1)} %copy-done, ...), custom_call_target="tpu_custom_call" | custom-call | tf_op jit(solution)/shard_map/pallas_call | solution.py:347
  55.5 1.0 %slice_convert_fusion = (f32[864,128]{1,0:T(8,128)}, f32[864,128]{1,0:T(8,128)}) fusion(bf16[896,128]{1,0:T(8,128)(2,1)S(1)} %bitcast.3, bf16[896,128]{1,0:T(8,128)(2,1)S(1)} %bitcast.2), kind=kLoop, calls=%fused_computation | loop fusion | flops 221184 | bytes 1327104 | tf_op jit(solution)/shard_map/convert_element_type | solution.py:404
  56.5 0.6 %copy.12 = bf16[1,8,2,16,128]{4,3,2,1,0:T(8,128)(2,1)} copy(bf16[1,8,2,16,128]{4,3,2,1,0:T(8,128)(2,1)S(1)} %get-tuple-element.14) | data formatting | bytes 131072
Async XLA Ops:
  1.9 1.2 %copy-start = (bf16[3456,128]{1,0:T(8,128)(2,1)S(1)}, bf16[3456,128]{1,0:T(8,128)(2,1)}, u32[]{:S(2)}) copy-start(bf16[3456,128]{1,0:T(8,128)(2,1)} %refs_2_.1) | copy-start | bytes 2654212
  3.1 1.2 %copy-start.1 = (bf16[3456,128]{1,0:T(8,128)(2,1)S(1)}, bf16[3456,128]{1,0:T(8,128)(2,1)}, u32[]{:S(2)}) copy-start(bf16[3456,128]{1,0:T(8,128)(2,1)} %refs_3_.1) | copy-start | bytes 2654212
  4.3 0.8 %copy-start.2 = (bf16[1,8,2,16,128]{4,3,2,1,0:T(8,128)(2,1)S(1)}, bf16[1,8,2,16,128]{4,3,2,1,0:T(8,128)(2,1)}, u32[]{:S(2)}) copy-start(bf16[1,8,2,16,128]{4,3,2,1,0:T(8,128)(2,1)} %refs_0_.1) | copy-start | bytes 196612
  5.1 0.8 %copy-start.3 = (bf16[1,8,2,16,128]{4,3,2,1,0:T(8,128)(2,1)S(1)}, bf16[1,8,2,16,128]{4,3,2,1,0:T(8,128)(2,1)}, u32[]{:S(2)}) copy-start(bf16[1,8,2,16,128]{4,3,2,1,0:T(8,128)(2,1)} %refs_1_.1) | copy-start | bytes 196612

commit v3 on v2

--- a/solution.py
+++ b/solution.py
@@ -20,6 +20,8 @@
 WIDTH = 128
 PLANE = ROWS * COLS
 SHARE = 864
+TILE = 16
+CHUNKS = (pl.ds(0, 64), pl.ds(64, 48))
 
 
 def shifted(value, step):
@@ -75,10 +77,10 @@
 
 def kernel(
     scale, video_ref, cotangent_ref, weight_one_ref, weight_two_ref, before_ref, count_ref,
-    output_ref, one_ref, two_ref,
-    first, second, ext_video, ext_delta, ext_hidden, cache, own_delta, next_delta, act, deltas,
-    part, swap_out, swap_in, total, stage, land_a, land_b, wide, other,
-    load, v_send, v_recv, vh_send, vh_recv, d_send, d_recv, dh_send, dh_recv, h_send, h_recv,
+    output_ref, grads_ref,
+    result_out, first, second, own_video, cotangent_in, ext_video, ext_delta, ext_hidden, cache, own_delta, next_delta, act, deltas,
+    part, swap_out, swap_in, total, stage, land_a, land_b, wide,
+    load, store, v_send, v_recv, vh_send, vh_recv, d_send, d_recv, dh_send, dh_recv, h_send, h_recv,
     swap_send, swap_recv, a_send, a_recv, b_send, b_recv, w_send, w_recv, o_send, o_recv,
 ):
     tm = lax.axis_index("tm")
@@ -122,24 +124,28 @@
         pltpu.make_async_copy(weight_one_ref, first, load.at[0]),
         pltpu.make_async_copy(weight_two_ref, second, load.at[1]),
     ]
-    for copy in loads:
+    video_load = pltpu.make_async_copy(video_ref.at[0], own_video, load.at[2])
+    cotangent_load = pltpu.make_async_copy(cotangent_ref.at[0], cotangent_in, load.at[3])
+    for copy in [video_load, cotangent_load] + loads:
         copy.start()
-    starting = before_ref[0] < 0
-    live = [jnp.where(count_ref[0] > frame, 1.0, 0.0) for frame in range(FRAMES)]
-    going = jnp.where(starting, 0.0, 1.0)
-    for frame in range(FRAMES):
-        masked = (live[frame] * cotangent_ref[0, frame].astype(FULL)).astype(HALF)
-        own_delta[frame] = masked
-        ext_delta[2 + frame, pl.ds(1 + LOW * space, LOW)] = masked
-        if frame < 2:
-            next_delta[frame] = (going * masked.astype(FULL)).astype(HALF)
     blank = jnp.zeros((COLS, WIDTH), HALF)
     for ref, frames in ((ext_video, 10), (ext_delta, 12), (ext_hidden, 10)):
         for frame in range(frames):
             ref[frame, 0] = blank
             ref[frame, ROWS + 1] = blank
     ext_delta[0:2] = jnp.zeros((2, ROWS + 2, COLS, WIDTH), HALF)
-    ext_video[2:, pl.ds(1 + LOW * space, LOW)] = video_ref[0]
+    starting = before_ref[0] < 0
+    live = [jnp.where(count_ref[0] > frame, 1.0, 0.0) for frame in range(FRAMES)]
+    going = jnp.where(starting, 0.0, 1.0)
+    cotangent_load.wait()
+    for frame in range(FRAMES):
+        masked = (live[frame] * cotangent_in[frame].astype(FULL)).astype(HALF)
+        own_delta[frame] = masked
+        ext_delta[2 + frame, pl.ds(1 + LOW * space, LOW)] = masked
+        if frame < 2:
+            next_delta[frame] = (going * masked.astype(FULL)).astype(HALF)
+    video_load.wait()
+    ext_video[2:, pl.ds(1 + LOW * space, LOW)] = own_video[...]
     pl.semaphore_wait(barrier, len(peers))
 
     sent = []
@@ -156,14 +162,14 @@
     place = pl.ds(1 + LOW * space, LOW)
     videos = [
         send(
-            video_ref.at[0], ext_video.at[pl.ds(2, FRAMES), place],
+            own_video, ext_video.at[pl.ds(2, FRAMES), place],
             v_send.at[step - 1], v_recv.at[step - 1], beside(step),
         )
         for step in range(1, SPACE)
     ]
     videos += [
         send(
-            video_ref.at[0, pl.ds(FRAMES - 2, 2)], ext_video.at[pl.ds(0, 2), place],
+            own_video.at[pl.ds(FRAMES - 2, 2)], ext_video.at[pl.ds(0, 2), place],
             vh_send.at[step], vh_recv.at[step], later(step),
         )
         for step in range(SPACE)
@@ -275,11 +281,15 @@
     total[SHARE:] = jnp.zeros((SIDE * BLOCK - SHARE, WIDTH), FULL)
     stage[...] = total[...].astype(HALF).reshape(stage.shape)
     over_a = []
-    for step in range(1, SIDE):
-        at, device = along_a(step)
-        over_a.append(
-            send(stage.at[at], land_a.at[step - 1], a_send.at[step - 1], a_recv.at[step - 1], device)
-        )
+    for number, chunk in enumerate(CHUNKS):
+        for step in range(1, SIDE):
+            at, device = along_a(step)
+            over_a.append(
+                send(
+                    stage.at[at, chunk], land_a.at[step - 1, chunk],
+                    a_send.at[number, step - 1], a_recv.at[number, step - 1], device,
+                )
+            )
 
     result = joined(
         jnp.dot(
@@ -288,47 +298,62 @@
         )
     ).reshape(FRAMES, LOW * COLS, WIDTH)
     for frame in range(FRAMES):
-        value = video_ref[0, frame].reshape(LOW * COLS, WIDTH).astype(FULL) + result[frame]
-        output_ref[0, frame] = (live[frame] * value).astype(HALF).reshape(LOW, COLS, WIDTH)
-
-    block = total[pl.ds(pl.multiple_of(a * BLOCK, BLOCK), BLOCK)]
-    for step in range(1, SIDE):
-        over_a[step - 1].wait_recv()
-        block = block + land_a[step - 1].astype(FULL)
-    land_b[b] = block.astype(HALF)
+        value = own_video[frame].reshape(LOW * COLS, WIDTH).astype(FULL) + result[frame]
+        result_out[frame] = (live[frame] * value).astype(HALF).reshape(LOW, COLS, WIDTH)
+    stores = [pltpu.make_async_copy(result_out, output_ref.at[0], store.at[0])]
+    stores[0].start()
+
     over_b = []
-    for step in range(1, SIDE):
-        over_b.append(
+    for number, chunk in enumerate(CHUNKS):
+        block = total[pl.ds(pl.multiple_of(a * BLOCK + chunk.start, TILE), chunk.size)]
+        for step in range(1, SIDE):
+            over_a[(SIDE - 1) * number + step - 1].wait_recv()
+            block = block + land_a[step - 1, chunk].astype(FULL)
+        land_b[b, chunk] = block.astype(HALF)
+        for step in range(1, SIDE):
+            over_b.append(
+                send(
+                    land_b.at[b, chunk], land_b.at[b, chunk],
+                    b_send.at[number, step - 1], b_recv.at[number, step - 1], along_b(step)[1],
+                )
+            )
+    back, across = [], []
+    for number, chunk in enumerate(CHUNKS):
+        for step in range(1, SIDE):
+            over_b[(SIDE - 1) * number + step - 1].wait_recv()
+        block = land_b[0, chunk].astype(FULL)
+        for at in range(1, SIDE):
+            block = block + land_b[at, chunk].astype(FULL)
+        wide[a, chunk] = (block * scale).astype(HALF)
+        for step in range(1, SIDE):
+            back.append(
+                send(
+                    wide.at[a, chunk], wide.at[a, chunk],
+                    w_send.at[number, step - 1], w_recv.at[number, step - 1], along_a(step)[1],
+                )
+            )
+        across.append(
             send(
-                land_b.at[b], land_b.at[b],
-                b_send.at[step - 1], b_recv.at[step - 1], along_b(step)[1],
-            )
-        )
-    for copy in over_b:
-        copy.wait_recv()
-    block = land_b[0].astype(FULL)
-    for at in range(1, SIDE):
-        block = block + land_b[at].astype(FULL)
-    wide[a] = (block * scale).astype(HALF)
-    back = []
-    for step in range(1, SIDE):
-        back.append(
-            send(
-                wide.at[a], wide.at[a],
-                w_send.at[step - 1], w_recv.at[step - 1], along_a(step)[1],
-            )
-        )
-    across = [send(wide.at[a], other.at[a], o_send.at[0], o_recv.at[0], sibling)]
-    for step in range(1, SIDE):
-        back[step - 1].wait_recv()
-        origin = lax.rem(a + SIDE - step, SIDE)
-        across.append(
-            send(wide.at[origin], other.at[origin], o_send.at[step], o_recv.at[step], sibling)
-        )
+                wide.at[a, chunk], grads_ref.at[core, a, chunk],
+                o_send.at[number, 0], o_recv.at[number, 0], sibling,
+            )
+        )
+    for number, chunk in enumerate(CHUNKS):
+        for step in range(1, SIDE):
+            back[(SIDE - 1) * number + step - 1].wait_recv()
+            origin = lax.rem(a + SIDE - step, SIDE)
+            across.append(
+                send(
+                    wide.at[origin, chunk], grads_ref.at[core, origin, chunk],
+                    o_send.at[number, step], o_recv.at[number, step], sibling,
+                )
+            )
+    stores.append(pltpu.make_async_copy(wide, grads_ref.at[core], store.at[1]))
+    stores[1].start()
     for copy in across:
         copy.wait_recv()
-    one_ref[...] = jnp.where(core == 0, wide[...], other[...])
-    two_ref[...] = jnp.where(core == 0, other[...], wide[...])
+    for copy in stores:
+        copy.wait()
     swap.wait_send()
     for copy in sent:
         copy.wait_send()
@@ -338,24 +363,24 @@
     frames, height, columns, width = video.shape[1:]
     groups, parts = lax.axis_size("tm"), lax.axis_size("space")
     scale = 1.0 / math.sqrt(groups * parts * frames * height * columns)
-    vmem = pl.BlockSpec(memory_space=pltpu.VMEM)
-    smem = pl.BlockSpec(memory_space=pltpu.SMEM)
-    anywhere = pl.BlockSpec(memory_space=pl.ANY)
+    far = pl.BlockSpec(memory_space=pltpu.HBM)
     dma = pltpu.SemaphoreType.DMA
     taps = weight_one.shape[0]
     blocks = (SIDE, BLOCK, WIDTH)
-    output, one, two = pl.pallas_call(
+    output, grads = pl.pallas_call(
         lambda *refs: kernel(scale, *refs),
         out_shape=(
             jax.ShapeDtypeStruct(video.shape, HALF),
-            jax.ShapeDtypeStruct(blocks, HALF),
-            jax.ShapeDtypeStruct(blocks, HALF),
+            jax.ShapeDtypeStruct((2,) + blocks, HALF),
         ),
-        in_specs=[vmem, vmem, anywhere, anywhere, smem, smem],
-        out_specs=(vmem, vmem, vmem),
+        in_specs=[far] * 4 + [pl.BlockSpec(memory_space=pltpu.SMEM)] * 2,
+        out_specs=(far, far),
         scratch_shapes=[
+            pltpu.VMEM((FRAMES, LOW, COLS, WIDTH), HALF),
             pltpu.VMEM((taps, WIDTH), HALF),
             pltpu.VMEM((taps, WIDTH), HALF),
+            pltpu.VMEM((FRAMES, LOW, COLS, WIDTH), HALF),
+            pltpu.VMEM((FRAMES, LOW, COLS, WIDTH), HALF),
             pltpu.VMEM((FRAMES + 2, ROWS + 2, COLS, WIDTH), HALF),
             pltpu.VMEM((FRAMES + 4, ROWS + 2, COLS, WIDTH), HALF),
             pltpu.VMEM((FRAMES + 2, ROWS + 2, COLS, WIDTH), HALF),
@@ -372,7 +397,7 @@
             pltpu.VMEM((SIDE - 1, BLOCK, WIDTH), HALF),
             pltpu.VMEM(blocks, HALF),
             pltpu.VMEM(blocks, HALF),
-            pltpu.VMEM(blocks, HALF),
+            dma((4,)),
             dma((2,)),
             dma((SPACE - 1,)),
             dma((SPACE - 1,)),
@@ -386,24 +411,27 @@
             dma,
             dma,
             dma,
-            dma((SIDE - 1,)),
-            dma((SIDE - 1,)),
-            dma((SIDE - 1,)),
-            dma((SIDE - 1,)),
-            dma((SIDE - 1,)),
-            dma((SIDE - 1,)),
-            dma((SIDE,)),
-            dma((SIDE,)),
+            dma((len(CHUNKS), SIDE - 1)),
+            dma((len(CHUNKS), SIDE - 1)),
+            dma((len(CHUNKS), SIDE - 1)),
+            dma((len(CHUNKS), SIDE - 1)),
+            dma((len(CHUNKS), SIDE - 1)),
+            dma((len(CHUNKS), SIDE - 1)),
+            dma((len(CHUNKS), SIDE)),
+            dma((len(CHUNKS), SIDE)),
         ],
         compiler_params=pltpu.CompilerParams(
-            collective_id=0, has_side_effects=True, vmem_limit_bytes=48 * 1024 * 1024
+            collective_id=0, has_side_effects=True, vmem_limit_bytes=62 * 1024 * 1024
         ),
     )(video, cotangent, weight_one, weight_two, predecessor, frame_count)
 
-    def widened(grad):
-        return grad.reshape(-1, WIDTH)[: taps // parts].astype(FULL)
-
-    return (output, widened(one), widened(two))
+    flat = grads.reshape(-1, WIDTH)
+
+    def widened(number):
+        begin = number * SIDE * BLOCK
+        return flat[begin : begin + taps // parts].astype(FULL)
+
+    return (output, widened(0), widened(1))
 
 
 def solution(mesh):

time: 57.4 us -> 54 us (0.941)
  local copies, waits for them, and re-layouts: 4.63 us -> 0.63 us
  other arithmetic: 0.97 us -> 2.04 us
    unnamed x9 -> x3, local copies, waits for them, and re-layouts: 4.63 us -> 0.63 us
    convert_element_type x1, other arithmetic: 0.97 us -> 2.04 us  [widened(): return flat[begin:begin + taps // parts].astype(FULL)]
where the time goes in v3:
time: 54 us; the launch traced here: 53.9 us
  Pallas kernels  49.2 us (91%)
  other arithmetic  2.04 us (4%)
  between operations  1.94 us (4%)
  local copies, waits for them, and re-layouts  0.63 us (1%)
    pallas_call x1, Pallas kernels, per_device(): pl.pallas_call(lambda *refs: kernel(scale, *refs), out_shape=(jax.ShapeDt...  49.2 us
    convert_element_type x1, other arithmetic, widened(): return flat[begin:begin + taps // parts].astype(FULL)  2.04 us

profile of v3, /device:TPU:1, one launch (start us, length us, event | category | flops | bytes accessed | tf_op | source)
XLA Modules:
  0.0 53.9 jit_solution(4612574632423988184)
XLA Ops:
  1.9 49.2 %shard_map.85 = (bf16[1,8,2,16,128]{4,3,2,1,0:T(8,128)(2,1)}, bf16[2,8,112,128]{3,2,1,0:T(8,128)(2,1)}) custom-call(bf16[1,8,2,16,128]{4,3,2,1,0:T(8,128)(2,1)} %refs_0_.1, bf16[1,8,2,16,128]{4,3,2,1,0:T(8,128)(2,1)} %refs_1_.1, bf16[3456,128]{1,0:T(8,128)(2,1)} %refs_2_.1, bf16[3456,128]{1,0:T(8,128)(2,1)} %refs_3_.1, s32[1]{0:T(128)S(6)} %copy.10.refs_4_, ...), custom_call_target="tpu_custom_call" | custom-call | tf_op jit(solution)/shard_map/pallas_call | solution.py:370
  51.2 0.0 copy-start
  51.2 2.0 %slice_convert_fusion = (f32[864,128]{1,0:T(8,128)}, f32[864,128]{1,0:T(8,128)}) fusion(bf16[1792,128]{1,0:T(8,128)(2,1)} %bitcast.1), kind=kLoop, calls=%fused_computation | loop fusion | flops 221184 | bytes 1327104 | tf_op jit(solution)/shard_map/convert_element_type | solution.py:432
  53.2 0.0 copy-done
  53.2 0.6 %copy.12 = bf16[1,8,2,16,128]{4,3,2,1,0:T(8,128)(2,1)} copy(bf16[1,8,2,16,128]{4,3,2,1,0:T(8,128)(2,1)S(1)} %copy-done) | data formatting | bytes 131072
Async XLA Ops:
  51.2 2.1 %copy-start = (bf16[1,8,2,16,128]{4,3,2,1,0:T(8,128)(2,1)S(1)}, bf16[1,8,2,16,128]{4,3,2,1,0:T(8,128)(2,1)}, u32[]{:S(2)}) copy-start(bf16[1,8,2,16,128]{4,3,2,1,0:T(8,128)(2,1)} %get-tuple-element.12) | copy-start | bytes 196612

commit v4 on v3

--- a/solution.py
+++ b/solution.py
@@ -78,7 +78,7 @@
 def kernel(
     scale, video_ref, cotangent_ref, weight_one_ref, weight_two_ref, before_ref, count_ref,
     output_ref, grads_ref,
-    result_out, first, second, own_video, cotangent_in, ext_video, ext_delta, ext_hidden, cache, own_delta, next_delta, act, deltas,
+    result_out, first, second, own_video, cotangent_in, ext_both, ext_delta, cache, own_delta, next_delta, slope, deltas,
     part, swap_out, swap_in, total, stage, land_a, land_b, wide,
     load, store, v_send, v_recv, vh_send, vh_recv, d_send, d_recv, dh_send, dh_recv, h_send, h_recv,
     swap_send, swap_recv, a_send, a_recv, b_send, b_recv, w_send, w_recv, o_send, o_recv,
@@ -113,13 +113,12 @@
     sibling = (tm + 1 - 2 * core, space)
 
     barrier = pltpu.get_barrier_semaphore()
-    peers = [beside(step) for step in range(1, SPACE)]
-    peers += [later(step) for step in range(SPACE)] + [earlier(step) for step in range(SPACE)]
-    peers += [along_a(step)[1] for step in range(1, SIDE)]
-    peers += [along_b(step)[1] for step in range(1, SIDE)]
-    for device in peers:
+    near = [beside(step) for step in range(1, SPACE)]
+    near += [later(step) for step in range(SPACE)] + [earlier(step) for step in range(SPACE)]
+    distant = [along_a(step)[1] for step in range(1, SIDE)]
+    distant += [along_b(step)[1] for step in range(1, SIDE)]
+    for device in near:
         pl.semaphore_signal(barrier, inc=1, device_id=device, device_id_type=MESH)
-
     loads = [
         pltpu.make_async_copy(weight_one_ref, first, load.at[0]),
         pltpu.make_async_copy(weight_two_ref, second, load.at[1]),
@@ -128,6 +127,10 @@
     cotangent_load = pltpu.make_async_copy(cotangent_ref.at[0], cotangent_in, load.at[3])
     for copy in [video_load, cotangent_load] + loads:
         copy.start()
+    for device in distant:
+        pl.semaphore_signal(barrier, inc=1, device_id=device, device_id_type=MESH)
+
+    ext_video, ext_hidden = ext_both.at[0], ext_both.at[1]
     blank = jnp.zeros((COLS, WIDTH), HALF)
     for ref, frames in ((ext_video, 10), (ext_delta, 12), (ext_hidden, 10)):
         for frame in range(frames):
@@ -146,9 +149,7 @@
             next_delta[frame] = (going * masked.astype(FULL)).astype(HALF)
     video_load.wait()
     ext_video[2:, pl.ds(1 + LOW * space, LOW)] = own_video[...]
-    pl.semaphore_wait(barrier, len(peers))
-
-    sent = []
+    pl.semaphore_wait(barrier, len(near) + len(distant))
 
     def send(source, target, send_sem, recv_sem, device):
         copy = pltpu.make_async_remote_copy(
@@ -156,7 +157,6 @@
             device_id=device, device_id_type=MESH,
         )
         copy.start()
-        sent.append(copy)
         return copy
 
     place = pl.ds(1 + LOW * space, LOW)
@@ -195,7 +195,7 @@
     for frame in range(2):
         ext_video[frame] = jnp.where(starting, ext_video[2], ext_video[frame])
 
-    act[...] = joined(
+    act = joined(
         jnp.dot(
             windows(ext_video, FRAMES, 0, ROWS), forward_weight(first),
             preferred_element_type=FULL,
@@ -203,7 +203,11 @@
     )
     for frame in range(FRAMES):
         value = act[frame * PLANE : (frame + 1) * PLANE]
-        hidden = (live[frame] * (value * jax.nn.sigmoid(value))).astype(HALF)
+        sigma = jax.nn.sigmoid(value)
+        hidden = (live[frame] * (value * sigma)).astype(HALF)
+        slope[frame * PLANE : (frame + 1) * PLANE] = live[frame] * (
+            sigma * (1.0 + value * (1.0 - sigma))
+        )
         ext_hidden[2 + frame, 1 : 1 + ROWS] = hidden.reshape(ROWS, COLS, WIDTH)
     passing = send(
         ext_hidden.at[pl.ds(FRAMES, 2), pl.ds(1, ROWS)], cache, h_send, h_recv, later(0)
@@ -228,39 +232,7 @@
         own = spread[(frame + 2) * PLANE : (frame + 3) * PLANE]
         if frame == 0:
             own = own + jnp.where(starting, spread[0:PLANE] + spread[PLANE : 2 * PLANE], 0.0)
-        value = act[frame * PLANE : (frame + 1) * PLANE]
-        sigma = jax.nn.sigmoid(value)
-        put(0, frame, own * live[frame] * (sigma * (1.0 + value * (1.0 - sigma))))
-
-    def gradient(slot, ref):
-        pieces = []
-        for step in range(3):
-            pair = 2 * space + step
-            pieces.append(
-                ref[pl.ds(pair // 3, FRAMES), pl.ds(lax.rem(pair, 3), ROWS)].reshape(-1, WIDTH)
-            )
-        term = lax.dot_general(
-            jnp.concatenate(pieces, axis=1), deltas[slot],
-            (((0,), (0,)), ((), ())), preferred_element_type=FULL,
-        )
-        for step in range(3):
-            for kw in range(3):
-                at = (3 * step + kw) * WIDTH
-                part[slot, at : at + WIDTH] = term[
-                    step * WIDTH : (step + 1) * WIDTH, kw * WIDTH : (kw + 1) * WIDTH
-                ]
-
-    share = pl.ds(pl.multiple_of(96 * space, 32), SHARE)
-    swap = pltpu.make_async_remote_copy(
-        src_ref=swap_out, dst_ref=swap_in, send_sem=swap_send, recv_sem=swap_recv,
-        device_id=sibling, device_id_type=MESH,
-    )
-    gradient(0, ext_video)
-
-    @pl.when(core == 1)
-    def _():
-        swap_out[...] = part[0, share].astype(HALF)
-        swap.start()
+        put(0, frame, own * slope[frame * PLANE : (frame + 1) * PLANE])
 
     for frame in range(FRAMES):
         put(1, frame, ext_delta[2 + frame, 1 : 1 + ROWS].reshape(PLANE, WIDTH).astype(FULL))
@@ -269,27 +241,54 @@
         ext_hidden[frame, 1 : 1 + ROWS] = jnp.where(
             starting, ext_hidden[2, 1 : 1 + ROWS], cache[frame]
         )
-    gradient(1, ext_hidden)
-
-    @pl.when(core == 0)
-    def _():
-        swap_out[...] = part[1, share].astype(HALF)
-        swap.start()
-
+
+    def gradient(slot):
+        pieces = []
+        for step in range(3):
+            pair = 2 * space + step
+            piece = ext_both[slot, pl.ds(pair // 3, FRAMES), pl.ds(lax.rem(pair, 3), ROWS)]
+            pieces.append(piece.reshape(-1, WIDTH))
+        term = lax.dot_general(
+            jnp.concatenate(pieces, axis=1), deltas[slot],
+            (((0,), (0,)), ((), ())), preferred_element_type=FULL,
+        )
+        for step in range(3):
+            for kw in range(3):
+                at = (3 * step + kw) * WIDTH
+                part[at : at + WIDTH] = term[
+                    step * WIDTH : (step + 1) * WIDTH, kw * WIDTH : (kw + 1) * WIDTH
+                ]
+        return part[pl.ds(pl.multiple_of(96 * space, 32), SHARE)]
+
+    swap_out[...] = gradient(1 - core).astype(HALF)
+    swap = send(swap_out, swap_in, swap_send, swap_recv, sibling)
+    total[0:SHARE] = gradient(core)
+    total[SHARE:] = jnp.zeros((SIDE * BLOCK - SHARE, WIDTH), FULL)
     swap.wait_recv()
-    total[0:SHARE] = part[core, share] + swap_in[...].astype(FULL)
-    total[SHARE:] = jnp.zeros((SIDE * BLOCK - SHARE, WIDTH), FULL)
+    total[0:SHARE] += swap_in[...].astype(FULL)
     stage[...] = total[...].astype(HALF).reshape(stage.shape)
-    over_a = []
-    for number, chunk in enumerate(CHUNKS):
+
+    def phase(number, chunk, source, target, send_sem, recv_sem, along):
         for step in range(1, SIDE):
-            at, device = along_a(step)
-            over_a.append(
-                send(
-                    stage.at[at, chunk], land_a.at[step - 1, chunk],
-                    a_send.at[number, step - 1], a_recv.at[number, step - 1], device,
-                )
-            )
+            at, device = along(step)
+            send(
+                source(at), target(step), send_sem.at[number], recv_sem.at[number], device
+            )
+        seven = land_a.at[pl.ds(0, SIDE - 1), chunk]
+        return (
+            pltpu.make_async_copy(seven, seven, send_sem.at[number]),
+            pltpu.make_async_copy(seven, seven, recv_sem.at[number]),
+        )
+
+    over_a = [
+        phase(
+            number, chunk, lambda at: stage.at[at, chunk], lambda step: land_a.at[step - 1, chunk],
+            a_send, a_recv, along_a,
+        )
+        for number, chunk in enumerate(CHUNKS)
+    ]
+    for copy in videos + changes + [passing, swap]:
+        copy.wait_send()
 
     result = joined(
         jnp.dot(
@@ -306,21 +305,21 @@
     over_b = []
     for number, chunk in enumerate(CHUNKS):
         block = total[pl.ds(pl.multiple_of(a * BLOCK + chunk.start, TILE), chunk.size)]
+        over_a[number][1].wait()
         for step in range(1, SIDE):
-            over_a[(SIDE - 1) * number + step - 1].wait_recv()
             block = block + land_a[step - 1, chunk].astype(FULL)
         land_b[b, chunk] = block.astype(HALF)
-        for step in range(1, SIDE):
-            over_b.append(
-                send(
-                    land_b.at[b, chunk], land_b.at[b, chunk],
-                    b_send.at[number, step - 1], b_recv.at[number, step - 1], along_b(step)[1],
-                )
-            )
+        over_b.append(
+            phase(
+                number, chunk, lambda at: land_b.at[b, chunk], lambda step: land_b.at[b, chunk],
+                b_send, b_recv, along_b,
+            )
+        )
+    for copy, _ in over_a:
+        copy.wait()
     back, across = [], []
     for number, chunk in enumerate(CHUNKS):
-        for step in range(1, SIDE):
-            over_b[(SIDE - 1) * number + step - 1].wait_recv()
+        over_b[number][1].wait()
         block = land_b[0, chunk].astype(FULL)
         for at in range(1, SIDE):
             block = block + land_b[at, chunk].astype(FULL)
@@ -338,6 +337,8 @@
                 o_send.at[number, 0], o_recv.at[number, 0], sibling,
             )
         )
+    for copy, _ in over_b:
+        copy.wait()
     for number, chunk in enumerate(CHUNKS):
         for step in range(1, SIDE):
             back[(SIDE - 1) * number + step - 1].wait_recv()
@@ -350,13 +351,12 @@
             )
     stores.append(pltpu.make_async_copy(wide, grads_ref.at[core], store.at[1]))
     stores[1].start()
+    for copy in back:
+        copy.wait_send()
     for copy in across:
-        copy.wait_recv()
+        copy.wait()
     for copy in stores:
         copy.wait()
-    swap.wait_send()
-    for copy in sent:
-        copy.wait_send()
 
 
 def per_device(video, cotangent, weight_one, weight_two, predecessor, frame_count):
@@ -381,15 +381,14 @@
             pltpu.VMEM((taps, WIDTH), HALF),
             pltpu.VMEM((FRAMES, LOW, COLS, WIDTH), HALF),
             pltpu.VMEM((FRAMES, LOW, COLS, WIDTH), HALF),
-            pltpu.VMEM((FRAMES + 2, ROWS + 2, COLS, WIDTH), HALF),
+            pltpu.VMEM((2, FRAMES + 2, ROWS + 2, COLS, WIDTH), HALF),
             pltpu.VMEM((FRAMES + 4, ROWS + 2, COLS, WIDTH), HALF),
-            pltpu.VMEM((FRAMES + 2, ROWS + 2, COLS, WIDTH), HALF),
             pltpu.VMEM((2, ROWS, COLS, WIDTH), HALF),
             pltpu.VMEM((FRAMES, LOW, COLS, WIDTH), HALF),
             pltpu.VMEM((2, LOW, COLS, WIDTH), HALF),
             pltpu.VMEM((FRAMES * PLANE, WIDTH), FULL),
             pltpu.VMEM((2, FRAMES * PLANE, 3 * WIDTH), HALF),
-            pltpu.VMEM((2, 9 * WIDTH, WIDTH), FULL),
+            pltpu.VMEM((9 * WIDTH, WIDTH), FULL),
             pltpu.VMEM((SHARE, WIDTH), HALF),
             pltpu.VMEM((SHARE, WIDTH), HALF),
             pltpu.VMEM((SIDE * BLOCK, WIDTH), FULL),
@@ -411,10 +410,10 @@
             dma,
             dma,
             dma,
-            dma((len(CHUNKS), SIDE - 1)),
-            dma((len(CHUNKS), SIDE - 1)),
-            dma((len(CHUNKS), SIDE - 1)),
-            dma((len(CHUNKS), SIDE - 1)),
+            dma((len(CHUNKS),)),
+            dma((len(CHUNKS),)),
+            dma((len(CHUNKS),)),
+            dma((len(CHUNKS),)),
             dma((len(CHUNKS), SIDE - 1)),
             dma((len(CHUNKS), SIDE - 1)),
             dma((len(CHUNKS), SIDE)),

time: 54 us -> 52.7 us (0.976)
  Pallas kernels: 49.2 us -> 47.9 us
    pallas_call x1, Pallas kernels: 49.2 us -> 47.9 us  [per_device(): pl.pallas_call(lambda *refs: kernel(scale, *refs), out_shape=(jax.ShapeDt...]
where the time goes in v4:
time: 52.7 us; the launch traced here: 52.5 us
  Pallas kernels  47.9 us (91%)
  other arithmetic  2.04 us (4%)
  between operations  1.94 us (4%)
  local copies, waits for them, and re-layouts  0.63 us (1%)
    pallas_call x1, Pallas kernels, per_device(): pl.pallas_call(lambda *refs: kernel(scale, *refs), out_shape=(jax.ShapeDt...  47.9 us
    convert_element_type x1, other arithmetic, widened(): return flat[begin:begin + taps // parts].astype(FULL)  2.04 us

profile of v4, /device:TPU:1, one launch (start us, length us, event | category | flops | bytes accessed | tf_op | source)
XLA Modules:
  0.0 52.5 jit_solution(4806825038300378598)
XLA Ops:
  1.9 47.9 %shard_map.85 = (bf16[1,8,2,16,128]{4,3,2,1,0:T(8,128)(2,1)}, bf16[2,8,112,128]{3,2,1,0:T(8,128)(2,1)}) custom-call(bf16[1,8,2,16,128]{4,3,2,1,0:T(8,128)(2,1)} %refs_0_.1, bf16[1,8,2,16,128]{4,3,2,1,0:T(8,128)(2,1)} %refs_1_.1, bf16[3456,128]{1,0:T(8,128)(2,1)} %refs_2_.1, bf16[3456,128]{1,0:T(8,128)(2,1)} %refs_3_.1, s32[1]{0:T(128)S(6)} %copy.10.refs_4_, ...), custom_call_target="tpu_custom_call" | custom-call | tf_op jit(solution)/shard_map/pallas_call | solution.py:370
  49.8 0.0 copy-start
  49.9 2.0 %slice_convert_fusion = (f32[864,128]{1,0:T(8,128)}, f32[864,128]{1,0:T(8,128)}) fusion(bf16[1792,128]{1,0:T(8,128)(2,1)} %bitcast.1), kind=kLoop, calls=%fused_computation | loop fusion | flops 221184 | bytes 1327104 | tf_op jit(solution)/shard_map/convert_element_type | solution.py:431
  51.9 0.0 copy-done
  51.9 0.6 %copy.12 = bf16[1,8,2,16,128]{4,3,2,1,0:T(8,128)(2,1)} copy(bf16[1,8,2,16,128]{4,3,2,1,0:T(8,128)(2,1)S(1)} %copy-done) | data formatting | bytes 131072
Async XLA Ops:
  49.8 2.1 %copy-start = (bf16[1,8,2,16,128]{4,3,2,1,0:T(8,128)(2,1)S(1)}, bf16[1,8,2,16,128]{4,3,2,1,0:T(8,128)(2,1)}, u32[]{:S(2)}) copy-start(bf16[1,8,2,16,128]{4,3,2,1,0:T(8,128)(2,1)} %get-tuple-element.12) | copy-start | bytes 196612

commit v5 on v4

--- a/solution.py
+++ b/solution.py
@@ -20,6 +20,7 @@
 WIDTH = 128
 PLANE = ROWS * COLS
 SHARE = 864
+FAR_FIRST = (4, 3, 5, 2, 6, 1, 7)
 TILE = 16
 CHUNKS = (pl.ds(0, 64), pl.ds(64, 48))
 
@@ -76,9 +77,9 @@
 
 
 def kernel(
-    scale, video_ref, cotangent_ref, weight_one_ref, weight_two_ref, before_ref, count_ref,
+    scale, video_ref, cotangent_ref, weight_one_ref, weight_two_ref, before_in, count_in,
     output_ref, grads_ref,
-    result_out, first, second, own_video, cotangent_in, ext_both, ext_delta, cache, own_delta, next_delta, slope, deltas,
+    before_ref, count_ref, result_out, first, second, own_video, cotangent_in, ext_both, ext_delta, cache, own_delta, next_delta, slope, deltas,
     part, swap_out, swap_in, total, stage, land_a, land_b, wide,
     load, store, v_send, v_recv, vh_send, vh_recv, d_send, d_recv, dh_send, dh_recv, h_send, h_recv,
     swap_send, swap_recv, a_send, a_recv, b_send, b_recv, w_send, w_recv, o_send, o_recv,
@@ -125,7 +126,11 @@
     ]
     video_load = pltpu.make_async_copy(video_ref.at[0], own_video, load.at[2])
     cotangent_load = pltpu.make_async_copy(cotangent_ref.at[0], cotangent_in, load.at[3])
-    for copy in [video_load, cotangent_load] + loads:
+    scalars = [
+        pltpu.make_async_copy(count_in, count_ref, load.at[4]),
+        pltpu.make_async_copy(before_in, before_ref, load.at[5]),
+    ]
+    for copy in scalars + [cotangent_load, video_load] + loads:
         copy.start()
     for device in distant:
         pl.semaphore_signal(barrier, inc=1, device_id=device, device_id_type=MESH)
@@ -137,8 +142,10 @@
             ref[frame, 0] = blank
             ref[frame, ROWS + 1] = blank
     ext_delta[0:2] = jnp.zeros((2, ROWS + 2, COLS, WIDTH), HALF)
-    starting = before_ref[0] < 0
-    live = [jnp.where(count_ref[0] > frame, 1.0, 0.0) for frame in range(FRAMES)]
+    for copy in scalars:
+        copy.wait()
+    starting = before_ref[0, 0] < 0
+    live = [jnp.where(count_ref[0, 0] > frame, 1.0, 0.0) for frame in range(FRAMES)]
     going = jnp.where(starting, 0.0, 1.0)
     cotangent_load.wait()
     for frame in range(FRAMES):
@@ -160,34 +167,35 @@
         return copy
 
     place = pl.ds(1 + LOW * space, LOW)
-    videos = [
-        send(
-            own_video, ext_video.at[pl.ds(2, FRAMES), place],
-            v_send.at[step - 1], v_recv.at[step - 1], beside(step),
-        )
-        for step in range(1, SPACE)
-    ]
-    videos += [
-        send(
-            own_video.at[pl.ds(FRAMES - 2, 2)], ext_video.at[pl.ds(0, 2), place],
-            vh_send.at[step], vh_recv.at[step], later(step),
-        )
-        for step in range(SPACE)
-    ]
-    changes = [
-        send(
-            own_delta, ext_delta.at[pl.ds(2, FRAMES), place],
-            d_send.at[step - 1], d_recv.at[step - 1], beside(step),
-        )
-        for step in range(1, SPACE)
-    ]
-    changes += [
-        send(
-            next_delta, ext_delta.at[pl.ds(2 + FRAMES, 2), place],
-            dh_send.at[step], dh_recv.at[step], earlier(step),
-        )
-        for step in range(SPACE)
-    ]
+    videos, changes = [], []
+    for step in (2, 1, 3, 0):
+        videos.append(
+            send(
+                own_video.at[pl.ds(FRAMES - 2, 2)], ext_video.at[pl.ds(0, 2), place],
+                vh_send.at[step], vh_recv.at[step], later(step),
+            )
+        )
+        if step:
+            videos.append(
+                send(
+                    own_video, ext_video.at[pl.ds(2, FRAMES), place],
+                    v_send.at[step - 1], v_recv.at[step - 1], beside(step),
+                )
+            )
+    for step in (2, 1, 3, 0):
+        changes.append(
+            send(
+                next_delta, ext_delta.at[pl.ds(2 + FRAMES, 2), place],
+                dh_send.at[step], dh_recv.at[step], earlier(step),
+            )
+        )
+        if step:
+            changes.append(
+                send(
+                    own_delta, ext_delta.at[pl.ds(2, FRAMES), place],
+                    d_send.at[step - 1], d_recv.at[step - 1], beside(step),
+                )
+            )
     for copy in loads:
         copy.wait()
     for copy in videos:
@@ -269,7 +277,7 @@
     stage[...] = total[...].astype(HALF).reshape(stage.shape)
 
     def phase(number, chunk, source, target, send_sem, recv_sem, along):
-        for step in range(1, SIDE):
+        for step in FAR_FIRST:
             at, device = along(step)
             send(
                 source(at), target(step), send_sem.at[number], recv_sem.at[number], device
@@ -317,38 +325,32 @@
         )
     for copy, _ in over_a:
         copy.wait()
-    back, across = [], []
+    back = []
     for number, chunk in enumerate(CHUNKS):
         over_b[number][1].wait()
         block = land_b[0, chunk].astype(FULL)
         for at in range(1, SIDE):
             block = block + land_b[at, chunk].astype(FULL)
         wide[a, chunk] = (block * scale).astype(HALF)
-        for step in range(1, SIDE):
+        for step in FAR_FIRST:
             back.append(
                 send(
                     wide.at[a, chunk], wide.at[a, chunk],
                     w_send.at[number, step - 1], w_recv.at[number, step - 1], along_a(step)[1],
                 )
             )
+    for copy, _ in over_b:
+        copy.wait()
+    across = []
+    for number, chunk in enumerate(CHUNKS):
+        for copy in back[(SIDE - 1) * number : (SIDE - 1) * (number + 1)]:
+            copy.wait_recv()
         across.append(
             send(
-                wide.at[a, chunk], grads_ref.at[core, a, chunk],
-                o_send.at[number, 0], o_recv.at[number, 0], sibling,
-            )
-        )
-    for copy, _ in over_b:
-        copy.wait()
-    for number, chunk in enumerate(CHUNKS):
-        for step in range(1, SIDE):
-            back[(SIDE - 1) * number + step - 1].wait_recv()
-            origin = lax.rem(a + SIDE - step, SIDE)
-            across.append(
-                send(
-                    wide.at[origin, chunk], grads_ref.at[core, origin, chunk],
-                    o_send.at[number, step], o_recv.at[number, step], sibling,
-                )
-            )
+                wide.at[:, chunk], grads_ref.at[core, :, chunk],
+                o_send.at[number], o_recv.at[number], sibling,
+            )
+        )
     stores.append(pltpu.make_async_copy(wide, grads_ref.at[core], store.at[1]))
     stores[1].start()
     for copy in back:
@@ -373,9 +375,11 @@
             jax.ShapeDtypeStruct(video.shape, HALF),
             jax.ShapeDtypeStruct((2,) + blocks, HALF),
         ),
-        in_specs=[far] * 4 + [pl.BlockSpec(memory_space=pltpu.SMEM)] * 2,
+        in_specs=[far] * 6,
         out_specs=(far, far),
         scratch_shapes=[
+            pltpu.SMEM((1, 1), jnp.int32),
+            pltpu.SMEM((1, 1), jnp.int32),
             pltpu.VMEM((FRAMES, LOW, COLS, WIDTH), HALF),
             pltpu.VMEM((taps, WIDTH), HALF),
             pltpu.VMEM((taps, WIDTH), HALF),
@@ -396,7 +400,7 @@
             pltpu.VMEM((SIDE - 1, BLOCK, WIDTH), HALF),
             pltpu.VMEM(blocks, HALF),
             pltpu.VMEM(blocks, HALF),
-            dma((4,)),
+            dma((6,)),
             dma((2,)),
             dma((SPACE - 1,)),
             dma((SPACE - 1,)),
@@ -416,13 +420,16 @@
             dma((len(CHUNKS),)),
             dma((len(CHUNKS), SIDE - 1)),
             dma((len(CHUNKS), SIDE - 1)),
-            dma((len(CHUNKS), SIDE)),
-            dma((len(CHUNKS), SIDE)),
+            dma((2,)),
+            dma((2,)),
         ],
         compiler_params=pltpu.CompilerParams(
             collective_id=0, has_side_effects=True, vmem_limit_bytes=62 * 1024 * 1024
         ),
-    )(video, cotangent, weight_one, weight_two, predecessor, frame_count)
+    )(
+        video, cotangent, weight_one, weight_two,
+        predecessor.reshape(1, 1), frame_count.reshape(1, 1),
+    )
 
     flat = grads.reshape(-1, WIDTH)
 

time: 52.7 us -> 51.5 us (0.977)
  Pallas kernels: 47.9 us -> 46.7 us
    pallas_call x1, Pallas kernels: 47.9 us -> 46.7 us  [per_device(): pl.pallas_call(lambda *refs: kernel(scale, *refs), out_shape=(jax.ShapeDt...]
where the time goes in v5:
time: 51.5 us; the launch traced here: 51.3 us
  Pallas kernels  46.7 us (91%)
  other arithmetic  2.04 us (4%)
  between operations  1.94 us (4%)
  local copies, waits for them, and re-layouts  0.63 us (1%)
    pallas_call x1, Pallas kernels, per_device(): pl.pallas_call(lambda *refs: kernel(scale, *refs), out_shape=(jax.ShapeDt...  46.7 us
    convert_element_type x1, other arithmetic, widened(): return flat[begin:begin + taps // parts].astype(FULL)  2.04 us

profile of v5, /device:TPU:1, one launch (start us, length us, event | category | flops | bytes accessed | tf_op | source)
XLA Modules:
  0.0 51.3 jit_solution(7823737496827998088)
XLA Ops:
  1.9 46.7 %shard_map.85 = (bf16[1,8,2,16,128]{4,3,2,1,0:T(8,128)(2,1)}, bf16[2,8,112,128]{3,2,1,0:T(8,128)(2,1)}) custom-call(bf16[1,8,2,16,128]{4,3,2,1,0:T(8,128)(2,1)} %refs_0_.1, bf16[1,8,2,16,128]{4,3,2,1,0:T(8,128)(2,1)} %refs_1_.1, bf16[3456,128]{1,0:T(8,128)(2,1)} %refs_2_.1, bf16[3456,128]{1,0:T(8,128)(2,1)} %refs_3_.1, s32[1,1]{1,0:T(1,128)} %bitcast.3.refs_4_, ...), custom_call_target="tpu_custom_call" | custom-call | tf_op jit(solution)/shard_map/pallas_call | solution.py:372
  48.7 0.0 copy-start
  48.7 2.0 %slice_convert_fusion = (f32[864,128]{1,0:T(8,128)}, f32[864,128]{1,0:T(8,128)}) fusion(bf16[1792,128]{1,0:T(8,128)(2,1)} %bitcast.5), kind=kLoop, calls=%fused_computation | loop fusion | flops 221184 | bytes 1327104 | tf_op jit(solution)/shard_map/convert_element_type | solution.py:438
  50.7 0.0 copy-done
  50.7 0.6 %copy.12 = bf16[1,8,2,16,128]{4,3,2,1,0:T(8,128)(2,1)} copy(bf16[1,8,2,16,128]{4,3,2,1,0:T(8,128)(2,1)S(1)} %copy-done) | data formatting | bytes 131072
Async XLA Ops:
  48.7 2.1 %copy-start = (bf16[1,8,2,16,128]{4,3,2,1,0:T(8,128)(2,1)S(1)}, bf16[1,8,2,16,128]{4,3,2,1,0:T(8,128)(2,1)}, u32[]{:S(2)}) copy-start(bf16[1,8,2,16,128]{4,3,2,1,0:T(8,128)(2,1)} %get-tuple-element.12) | copy-start | bytes 196612

commit v6 on v5

--- a/solution.py
+++ b/solution.py
@@ -37,10 +37,10 @@
     return middle + shifted(left, 1) + shifted(right, -1)
 
 
-def windows(ref, frames, start, height):
+def windows(ref, begin, frames, start, height):
     return jnp.concatenate(
         [
-            ref[kt : kt + frames, pl.ds(start + kh, height)].reshape(-1, WIDTH)
+            ref[begin + kt : begin + kt + frames, pl.ds(start + kh, height)].reshape(-1, WIDTH)
             for kt in range(3)
             for kh in range(3)
         ],
@@ -182,20 +182,20 @@
                     v_send.at[step - 1], v_recv.at[step - 1], beside(step),
                 )
             )
-    for step in (2, 1, 3, 0):
+    for step in (2, 1, 3):
         changes.append(
             send(
-                next_delta, ext_delta.at[pl.ds(2 + FRAMES, 2), place],
-                dh_send.at[step], dh_recv.at[step], earlier(step),
-            )
-        )
-        if step:
-            changes.append(
-                send(
-                    own_delta, ext_delta.at[pl.ds(2, FRAMES), place],
-                    d_send.at[step - 1], d_recv.at[step - 1], beside(step),
-                )
-            )
+                own_delta, ext_delta.at[pl.ds(2, FRAMES), place],
+                d_send.at[step - 1], d_recv.at[step - 1], beside(step),
+            )
+        )
+    following = [
+        send(
+            next_delta, ext_delta.at[pl.ds(2 + FRAMES, 2), place],
+            dh_send.at[step], dh_recv.at[step], earlier(step),
+        )
+        for step in (2, 1, 3, 0)
+    ]
     for copy in loads:
         copy.wait()
     for copy in videos:
@@ -203,33 +203,28 @@
     for frame in range(2):
         ext_video[frame] = jnp.where(starting, ext_video[2], ext_video[frame])
 
-    act = joined(
-        jnp.dot(
-            windows(ext_video, FRAMES, 0, ROWS), forward_weight(first),
-            preferred_element_type=FULL,
-        )
-    )
-    for frame in range(FRAMES):
-        value = act[frame * PLANE : (frame + 1) * PLANE]
-        sigma = jax.nn.sigmoid(value)
-        hidden = (live[frame] * (value * sigma)).astype(HALF)
-        slope[frame * PLANE : (frame + 1) * PLANE] = live[frame] * (
-            sigma * (1.0 + value * (1.0 - sigma))
-        )
-        ext_hidden[2 + frame, 1 : 1 + ROWS] = hidden.reshape(ROWS, COLS, WIDTH)
+    weight = forward_weight(first)
+    count = FRAMES // 2
+    for begin in range(0, FRAMES, count):
+        act = joined(
+            jnp.dot(
+                windows(ext_video, begin, count, 0, ROWS), weight, preferred_element_type=FULL
+            )
+        )
+        for frame in range(begin, begin + count):
+            value = act[(frame - begin) * PLANE : (frame - begin + 1) * PLANE]
+            sigma = jax.nn.sigmoid(value)
+            hidden = (live[frame] * (value * sigma)).astype(HALF)
+            slope[frame * PLANE : (frame + 1) * PLANE] = live[frame] * (
+                sigma * (1.0 + value * (1.0 - sigma))
+            )
+            ext_hidden[2 + frame, 1 : 1 + ROWS] = hidden.reshape(ROWS, COLS, WIDTH)
     passing = send(
         ext_hidden.at[pl.ds(FRAMES, 2), pl.ds(1, ROWS)], cache, h_send, h_recv, later(0)
     )
 
     for copy in changes:
         copy.wait_recv()
-    spread = joined(
-        lax.dot_general(
-            windows(ext_delta, FRAMES + 2, 0, ROWS), backward_weight(second),
-            (((1,), (1,)), ((), ())), preferred_element_type=FULL,
-        )
-    )
-
     def put(slot, frame, value):
         at = slice(frame * PLANE, (frame + 1) * PLANE)
         deltas[slot, at, 0:WIDTH] = shifted(value, -1).astype(HALF)
@@ -237,13 +232,28 @@
         deltas[slot, at, 2 * WIDTH :] = shifted(value, 1).astype(HALF)
 
     for frame in range(FRAMES):
-        own = spread[(frame + 2) * PLANE : (frame + 3) * PLANE]
-        if frame == 0:
-            own = own + jnp.where(starting, spread[0:PLANE] + spread[PLANE : 2 * PLANE], 0.0)
-        put(0, frame, own * slope[frame * PLANE : (frame + 1) * PLANE])
-
-    for frame in range(FRAMES):
         put(1, frame, ext_delta[2 + frame, 1 : 1 + ROWS].reshape(PLANE, WIDTH).astype(FULL))
+    weight = backward_weight(second)
+    count = (FRAMES + 2) // 2
+    early = 0.0
+    for begin in range(0, FRAMES + 2, count):
+        if begin:
+            for copy in following:
+                copy.wait_recv()
+        spread = joined(
+            lax.dot_general(
+                windows(ext_delta, begin, count, 0, ROWS), weight,
+                (((1,), (1,)), ((), ())), preferred_element_type=FULL,
+            )
+        )
+        for frame in range(begin, begin + count):
+            own = spread[(frame - begin) * PLANE : (frame - begin + 1) * PLANE]
+            if frame < 2:
+                early = early + own
+                continue
+            if frame == 2:
+                own = own + jnp.where(starting, early, 0.0)
+            put(0, frame - 2, own * slope[(frame - 2) * PLANE : (frame - 1) * PLANE])
     passing.wait_recv()
     for frame in range(2):
         ext_hidden[frame, 1 : 1 + ROWS] = jnp.where(
@@ -295,12 +305,12 @@
         )
         for number, chunk in enumerate(CHUNKS)
     ]
-    for copy in videos + changes + [passing, swap]:
+    for copy in videos + changes + following + [passing, swap]:
         copy.wait_send()
 
     result = joined(
         jnp.dot(
-            windows(ext_hidden, FRAMES, LOW * space, LOW), forward_weight(second),
+            windows(ext_hidden, 0, FRAMES, LOW * space, LOW), forward_weight(second),
             preferred_element_type=FULL,
         )
     ).reshape(FRAMES, LOW * COLS, WIDTH)

time: 51.5 us -> 51.4 us (level)
  no operation moved by 1% of the time
where the time goes in v6:
time: 51.4 us; the launch traced here: 51.2 us
  Pallas kernels  46.6 us (91%)
  other arithmetic  2.04 us (4%)
  between operations  1.94 us (4%)
  local copies, waits for them, and re-layouts  0.63 us (1%)
    pallas_call x1, Pallas kernels, per_device(): pl.pallas_call(lambda *refs: kernel(scale, *refs), out_shape=(jax.ShapeDt...  46.6 us
    convert_element_type x1, other arithmetic, widened(): return flat[begin:begin + taps // parts].astype(FULL)  2.04 us

profile of v6, /device:TPU:1, one launch (start us, length us, event | category | flops | bytes accessed | tf_op | source)
XLA Modules:
  0.0 51.2 jit_solution(14540035681792136491)
XLA Ops:
  1.9 46.6 %shard_map.85 = (bf16[1,8,2,16,128]{4,3,2,1,0:T(8,128)(2,1)}, bf16[2,8,112,128]{3,2,1,0:T(8,128)(2,1)}) custom-call(bf16[1,8,2,16,128]{4,3,2,1,0:T(8,128)(2,1)} %refs_0_.1, bf16[1,8,2,16,128]{4,3,2,1,0:T(8,128)(2,1)} %refs_1_.1, bf16[3456,128]{1,0:T(8,128)(2,1)} %refs_2_.1, bf16[3456,128]{1,0:T(8,128)(2,1)} %refs_3_.1, s32[1,1]{1,0:T(1,128)} %bitcast.3.refs_4_, ...), custom_call_target="tpu_custom_call" | custom-call | tf_op jit(solution)/shard_map/pallas_call | solution.py:382
  48.5 0.0 copy-start
  48.5 2.0 %slice_convert_fusion = (f32[864,128]{1,0:T(8,128)}, f32[864,128]{1,0:T(8,128)}) fusion(bf16[1792,128]{1,0:T(8,128)(2,1)} %bitcast.5), kind=kLoop, calls=%fused_computation | loop fusion | flops 221184 | bytes 1327104 | tf_op jit(solution)/shard_map/convert_element_type | solution.py:448
  50.6 0.0 copy-done
  50.6 0.6 %copy.12 = bf16[1,8,2,16,128]{4,3,2,1,0:T(8,128)(2,1)} copy(bf16[1,8,2,16,128]{4,3,2,1,0:T(8,128)(2,1)S(1)} %copy-done) | data formatting | bytes 131072
Async XLA Ops:
  48.5 2.1 %copy-start = (bf16[1,8,2,16,128]{4,3,2,1,0:T(8,128)(2,1)S(1)}, bf16[1,8,2,16,128]{4,3,2,1,0:T(8,128)(2,1)}, u32[]{:S(2)}) copy-start(bf16[1,8,2,16,128]{4,3,2,1,0:T(8,128)(2,1)} %get-tuple-element.12) | copy-start | bytes 196612

commit v7 on v6

--- a/solution.py
+++ b/solution.py
@@ -22,7 +22,7 @@
 SHARE = 864
 FAR_FIRST = (4, 3, 5, 2, 6, 1, 7)
 TILE = 16
-CHUNKS = (pl.ds(0, 64), pl.ds(64, 48))
+CHUNKS = (pl.ds(0, 48), pl.ds(48, 64))
 
 
 def shifted(value, step):

time: 51.4 us -> 51.3 us (level)
  no operation moved by 1% of the time
where the time goes in v7:
time: 51.3 us; the launch traced here: 51.1 us
  Pallas kernels  46.5 us (91%)
  other arithmetic  2.04 us (4%)
  between operations  1.94 us (4%)
  local copies, waits for them, and re-layouts  0.63 us (1%)
    pallas_call x1, Pallas kernels, per_device(): pl.pallas_call(lambda *refs: kernel(scale, *refs), out_shape=(jax.ShapeDt...  46.5 us
    convert_element_type x1, other arithmetic, widened(): return flat[begin:begin + taps // parts].astype(FULL)  2.04 us

profile of v7, /device:TPU:1, one launch (start us, length us, event | category | flops | bytes accessed | tf_op | source)
XLA Modules:
  0.0 51.1 jit_solution(16102776957760107983)
XLA Ops:
  1.9 46.5 %shard_map.85 = (bf16[1,8,2,16,128]{4,3,2,1,0:T(8,128)(2,1)}, bf16[2,8,112,128]{3,2,1,0:T(8,128)(2,1)}) custom-call(bf16[1,8,2,16,128]{4,3,2,1,0:T(8,128)(2,1)} %refs_0_.1, bf16[1,8,2,16,128]{4,3,2,1,0:T(8,128)(2,1)} %refs_1_.1, bf16[3456,128]{1,0:T(8,128)(2,1)} %refs_2_.1, bf16[3456,128]{1,0:T(8,128)(2,1)} %refs_3_.1, s32[1,1]{1,0:T(1,128)} %bitcast.3.refs_4_, ...), custom_call_target="tpu_custom_call" | custom-call | tf_op jit(solution)/shard_map/pallas_call | solution.py:382
  48.5 0.0 copy-start
  48.5 2.0 %slice_convert_fusion = (f32[864,128]{1,0:T(8,128)}, f32[864,128]{1,0:T(8,128)}) fusion(bf16[1792,128]{1,0:T(8,128)(2,1)} %bitcast.5), kind=kLoop, calls=%fused_computation | loop fusion | flops 221184 | bytes 1327104 | tf_op jit(solution)/shard_map/convert_element_type | solution.py:448
  50.5 0.0 copy-done
  50.5 0.6 %copy.12 = bf16[1,8,2,16,128]{4,3,2,1,0:T(8,128)(2,1)} copy(bf16[1,8,2,16,128]{4,3,2,1,0:T(8,128)(2,1)S(1)} %copy-done) | data formatting | bytes 131072
Async XLA Ops:
  48.5 2.1 %copy-start = (bf16[1,8,2,16,128]{4,3,2,1,0:T(8,128)(2,1)S(1)}, bf16[1,8,2,16,128]{4,3,2,1,0:T(8,128)(2,1)}, u32[]{:S(2)}) copy-start(bf16[1,8,2,16,128]{4,3,2,1,0:T(8,128)(2,1)} %get-tuple-element.12) | copy-start | bytes 196612
